TPU v7x, 32 devices: a whole 2x2x4 slice. The times are simulated.
32 devices in a mesh: rows: 8 (over z, core), feat: 4 (over y, x).
Axes of the slice: x: 2, y: 2, z: 4, core: 2. Of those that a mesh axis runs over, the one named last changes fastest.
Arguments:
- features: bfloat16 [8192, 4096], P('rows', 'feat'), may hold values from -0.0625 to 0.0625
- inverse_gram: float32 [4096, 1024], P('feat'), as said below
- targets: float32 [128, 8192], P('feat', 'rows'), may hold values from -6 to 6
Outputs:
- weights: float32 [128, 4096], P(None, 'feat')
- residual: float32 [128, 8192], P('feat', 'rows')
Inputs may be any that keep to these rules, and one draw needn't show every extreme that they name: Each block of inverse_gram is symmetric.
All inputs are finite; a program needn't handle non-finite values.
Results may differ from a plain program's by a relative error of at most 0.007.
Values sent between devices are 32-bit elements; how exact they have to be, the bound alone decides.
A program may use at most 64 MiB of HBM per device.

v0:
```python
import jax
import jax.numpy as jnp
from jax import lax
from jax.sharding import PartitionSpec as P

TGT = 128
TURNS = 2


ridge_weight = 0.5


def passed_along(block, axis, distance):
    devices = range(lax.axis_size(axis))
    route = [((i - distance) % len(devices), i) for i in devices]
    return lax.ppermute(block, axis, route)


def local(features, inverse_gram, targets):
    block_count = lax.axis_size("feat")
    position = lax.axis_index("feat")
    panel_width = targets.shape[0]

    def refine(panel_rows, panel_weights):
        partial_value = jnp.dot(
            panel_rows.astype(jnp.bfloat16), features, preferred_element_type=jnp.float32
        )
        projection = lax.psum(partial_value, "rows")
        increment = jnp.dot(
            projection - ridge_weight * panel_weights, inverse_gram, precision=lax.Precision.HIGHEST
        )
        fitted = lax.dot_general(
            increment.astype(jnp.bfloat16),
            features,
            (((1,), (1,)), ((), ())),
            preferred_element_type=jnp.float32,
        )
        return (panel_rows - fitted, panel_weights + increment)

    def advance(section, carried):
        residual, weights = carried
        panel_index = (position - section) % block_count
        start = panel_index * panel_width
        panel_weights = lax.dynamic_slice_in_dim(weights, start, panel_width, 0)
        residual, panel_weights = refine(residual, panel_weights)
        weights = lax.dynamic_update_slice_in_dim(weights, panel_weights, start, 0)
        residual = passed_along(residual, "feat", 1)
        return (residual, weights)

    carried = (targets, jnp.zeros((TGT, features.shape[1]), jnp.float32))
    for sweep_index in range(TURNS):
        offset = sweep_index * block_count

        def sweep_step(inner, state, offset=offset):
            return advance(inner + offset, state)

        carried = lax.fori_loop(0, block_count, sweep_step, carried)
    residual, weights = carried
    return (weights, residual)


def solution(mesh):
    placed = (P("rows", "feat"), P("feat", None), P("feat", "rows"))
    return jax.shard_map(
        local,
        mesh=mesh,
        in_specs=placed,
        out_specs=(P(None, "feat"), P("feat", "rows")),
        check_vma=False,
    )
```

profile of v0, /device:TPU:0, one launch (start us, length us, event | category | flops | bytes accessed | tf_op | source)
XLA Modules:
  0.0 560.9 jit_solution(14350422905588079473)
XLA Ops:
  7.2 0.9 copy.29
  8.1 274.7 %while.34 = (s32[]{:T(128)}, f32[32,1024]{1,0:T(8,128)S(1)}, f32[128,1024]{1,0:T(8,128)S(1)}, bf16[1024,1024]{1,0:T(8,128)(2,1)}, s32[]{:T(128)}, /*index=5*/f32...) while((s32[]{:T(128)}, f32[32,1024]{1,0:T(8,128)S(1)}, ...), condition=%wide.region_2.3_spmd, body=%wide.region_0.2_spmd.sunk | while | flops 537100288 | bytes 19530128 | solution.py:57
  8.2 2.7 fusion.48
  10.9 57.8 %all-reduce.3.cloned.1.call-done = f32[32,1024]{1,0:T(8,128)} async-done(((f32[32,1024]{1,0:T(8,128)}), f32[32,1024]{1,0:T(8,128)}) %all-reduce.3.cloned.1.call-update) | async-done | bytes 131088 | tf_op jit(solution)/shard_map/while/body/eval_jaxpr/psum | solution.py:28
  68.8 4.9 fusion.49
  73.7 0.7 convolution_subtract_fusion.4
  74.4 1.5 collective-permute-start
  75.9 4.4 collective-permute-done
  80.3 2.7 fusion.48
  83.1 53.3 %all-reduce.3.cloned.1.call-done = f32[32,1024]{1,0:T(8,128)} async-done(((f32[32,1024]{1,0:T(8,128)}), f32[32,1024]{1,0:T(8,128)}) %all-reduce.3.cloned.1.call-update) | async-done | bytes 131088 | tf_op jit(solution)/shard_map/while/body/eval_jaxpr/psum | solution.py:28
  136.4 4.9 fusion.49
  142.0 1.5 collective-permute-start
  143.6 4.4 collective-permute-done
  147.9 2.7 fusion.48
  150.7 53.3 %all-reduce.3.cloned.1.call-done = f32[32,1024]{1,0:T(8,128)} async-done(((f32[32,1024]{1,0:T(8,128)}), f32[32,1024]{1,0:T(8,128)}) %all-reduce.3.cloned.1.call-update) | async-done | bytes 131088 | tf_op jit(solution)/shard_map/while/body/eval_jaxpr/psum | solution.py:28
  204.0 4.9 fusion.49
  208.9 0.7 convolution_subtract_fusion.4
  209.6 1.5 collective-permute-start
  211.2 4.4 collective-permute-done
  215.5 2.7 fusion.48
  218.3 53.0 %all-reduce.3.cloned.1.call-done = f32[32,1024]{1,0:T(8,128)} async-done(((f32[32,1024]{1,0:T(8,128)}), f32[32,1024]{1,0:T(8,128)}) %all-reduce.3.cloned.1.call-update) | async-done | bytes 131088 | tf_op jit(solution)/shard_map/while/body/eval_jaxpr/psum | solution.py:28
  271.3 4.9 fusion.49
  276.9 1.5 collective-permute-start
  278.5 4.4 collective-permute-done
  282.8 270.3 %while.35 = (s32[]{:T(128)}, f32[32,1024]{1,0:T(8,128)S(1)}, f32[128,1024]{1,0:T(8,128)S(1)}, bf16[1024,1024]{1,0:T(8,128)(2,1)}, s32[]{:T(128)}, /*index=5*/f32...) while((s32[]{:T(128)}, f32[32,1024]{1,0:T(8,128)S(1)}, ...), condition=%wide.region_5.6_spmd, body=%wide.region_3.5_spmd.sunk | while | flops 537100288 | bytes 19530140 | solution.py:57
  282.8 2.7 fusion.56
  285.6 53.1 %all-reduce.5.cloned.1.call-done = f32[32,1024]{1,0:T(8,128)} async-done(((f32[32,1024]{1,0:T(8,128)}), f32[32,1024]{1,0:T(8,128)}) %all-reduce.5.cloned.1.call-update) | async-done | bytes 131088 | tf_op jit(solution)/shard_map/while/body/eval_jaxpr/psum | solution.py:28
  338.7 4.9 fusion.57
  343.6 0.7 convolution_subtract_fusion.5
  344.4 1.5 collective-permute-start.1
  345.9 4.4 collective-permute-done.1
  350.3 2.7 fusion.56
  353.0 53.1 %all-reduce.5.cloned.1.call-done = f32[32,1024]{1,0:T(8,128)} async-done(((f32[32,1024]{1,0:T(8,128)}), f32[32,1024]{1,0:T(8,128)}) %all-reduce.5.cloned.1.call-update) | async-done | bytes 131088 | tf_op jit(solution)/shard_map/while/body/eval_jaxpr/psum | solution.py:28
  406.2 4.9 fusion.57
  411.1 0.7 convolution_subtract_fusion.5
  411.8 1.5 collective-permute-start.1
  413.3 4.4 collective-permute-done.1
  417.7 2.7 fusion.56
  420.5 53.4 %all-reduce.5.cloned.1.call-done = f32[32,1024]{1,0:T(8,128)} async-done(((f32[32,1024]{1,0:T(8,128)}), f32[32,1024]{1,0:T(8,128)}) %all-reduce.5.cloned.1.call-update) | async-done | bytes 131088 | tf_op jit(solution)/shard_map/while/body/eval_jaxpr/psum | solution.py:28
  473.9 4.9 fusion.57
  478.8 0.7 convolution_subtract_fusion.5
  479.5 1.5 collective-permute-start.1
  481.1 4.4 collective-permute-done.1
  485.4 2.7 fusion.56
  488.2 53.4 %all-reduce.5.cloned.1.call-done = f32[32,1024]{1,0:T(8,128)} async-done(((f32[32,1024]{1,0:T(8,128)}), f32[32,1024]{1,0:T(8,128)}) %all-reduce.5.cloned.1.call-update) | async-done | bytes 131088 | tf_op jit(solution)/shard_map/while/body/eval_jaxpr/psum | solution.py:28
  541.7 4.9 fusion.57
  547.3 1.5 collective-permute-start.1
  548.8 4.4 collective-permute-done.1
  (47 shorter events, 3.4 us)
Async XLA Ops:
  8.1 60.6 %all-reduce.3.cloned.1.call-start = ((), (), s32[]{:S(2)}) async-start(), calls=%async_computation | async-start | bytes 262144 | tf_op jit(solution)/shard_map/while/body/eval_jaxpr/psum | solution.py:28
  68.8 4.9 copy-start
  74.4 5.9 %collective-permute-start = (f32[32,1024]{1,0:T(8,128)S(1)}, f32[32,1024]{1,0:T(8,128)S(1)}, u32[]{:S(2)}, u32[]{:S(2)}) collective-permute-start(f32[32,1024]{1,0:T(8,128)S(1)} %convolution_subtract_fusion.4), channel_id=1, source_target_pairs={{3,0},{0,1},{1,2},{2,3},{7,4},{4,5},{5,6},{6,7},{11,8},{8,9},{9,10... | collective-permute-start | bytes 393224 | tf_op jit(solution)/shard_map/while/body/eval_jaxpr/ppermute | solution.py:16
  80.3 56.1 %all-reduce.3.cloned.1.call-start = ((), (), s32[]{:S(2)}) async-start(), calls=%async_computation | async-start | bytes 262144 | tf_op jit(solution)/shard_map/while/body/eval_jaxpr/psum | solution.py:28
  136.4 4.9 copy-start
  142.0 5.9 %collective-permute-start = (f32[32,1024]{1,0:T(8,128)S(1)}, f32[32,1024]{1,0:T(8,128)S(1)}, u32[]{:S(2)}, u32[]{:S(2)}) collective-permute-start(f32[32,1024]{1,0:T(8,128)S(1)} %convolution_subtract_fusion.4), channel_id=1, source_target_pairs={{3,0},{0,1},{1,2},{2,3},{7,4},{4,5},{5,6},{6,7},{11,8},{8,9},{9,10... | collective-permute-start | bytes 393224 | tf_op jit(solution)/shard_map/while/body/eval_jaxpr/ppermute | solution.py:16
  147.9 56.1 %all-reduce.3.cloned.1.call-start = ((), (), s32[]{:S(2)}) async-start(), calls=%async_computation | async-start | bytes 262144 | tf_op jit(solution)/shard_map/while/body/eval_jaxpr/psum | solution.py:28
  204.0 4.9 copy-start
  209.6 5.9 %collective-permute-start = (f32[32,1024]{1,0:T(8,128)S(1)}, f32[32,1024]{1,0:T(8,128)S(1)}, u32[]{:S(2)}, u32[]{:S(2)}) collective-permute-start(f32[32,1024]{1,0:T(8,128)S(1)} %convolution_subtract_fusion.4), channel_id=1, source_target_pairs={{3,0},{0,1},{1,2},{2,3},{7,4},{4,5},{5,6},{6,7},{11,8},{8,9},{9,10... | collective-permute-start | bytes 393224 | tf_op jit(solution)/shard_map/while/body/eval_jaxpr/ppermute | solution.py:16
  215.5 55.8 %all-reduce.3.cloned.1.call-start = ((), (), s32[]{:S(2)}) async-start(), calls=%async_computation | async-start | bytes 262144 | tf_op jit(solution)/shard_map/while/body/eval_jaxpr/psum | solution.py:28
  271.3 4.9 copy-start
  276.9 5.9 %collective-permute-start = (f32[32,1024]{1,0:T(8,128)S(1)}, f32[32,1024]{1,0:T(8,128)S(1)}, u32[]{:S(2)}, u32[]{:S(2)}) collective-permute-start(f32[32,1024]{1,0:T(8,128)S(1)} %convolution_subtract_fusion.4), channel_id=1, source_target_pairs={{3,0},{0,1},{1,2},{2,3},{7,4},{4,5},{5,6},{6,7},{11,8},{8,9},{9,10... | collective-permute-start | bytes 393224 | tf_op jit(solution)/shard_map/while/body/eval_jaxpr/ppermute | solution.py:16
  282.8 55.9 %all-reduce.5.cloned.1.call-start = ((), (), s32[]{:S(2)}) async-start(), calls=%async_computation.1 | async-start | bytes 262144 | tf_op jit(solution)/shard_map/while/body/eval_jaxpr/psum | solution.py:28
  338.7 4.9 copy-start.1
  344.4 5.9 %collective-permute-start.1 = (f32[32,1024]{1,0:T(8,128)S(1)}, f32[32,1024]{1,0:T(8,128)S(1)}, u32[]{:S(2)}, u32[]{:S(2)}) collective-permute-start(f32[32,1024]{1,0:T(8,128)S(1)} %convolution_subtract_fusion.5), channel_id=1, source_target_pairs={{3,0},{0,1},{1,2},{2,3},{7,4},{4,5},{5,6},{6,7},{11,8},{8,9},{9,10... | collective-permute-start | bytes 393224 | tf_op jit(solution)/shard_map/while/body/eval_jaxpr/ppermute | solution.py:16
  350.3 55.9 %all-reduce.5.cloned.1.call-start = ((), (), s32[]{:S(2)}) async-start(), calls=%async_computation.1 | async-start | bytes 262144 | tf_op jit(solution)/shard_map/while/body/eval_jaxpr/psum | solution.py:28
  406.2 4.9 copy-start.1
  411.8 5.9 %collective-permute-start.1 = (f32[32,1024]{1,0:T(8,128)S(1)}, f32[32,1024]{1,0:T(8,128)S(1)}, u32[]{:S(2)}, u32[]{:S(2)}) collective-permute-start(f32[32,1024]{1,0:T(8,128)S(1)} %convolution_subtract_fusion.5), channel_id=1, source_target_pairs={{3,0},{0,1},{1,2},{2,3},{7,4},{4,5},{5,6},{6,7},{11,8},{8,9},{9,10... | collective-permute-start | bytes 393224 | tf_op jit(solution)/shard_map/while/body/eval_jaxpr/ppermute | solution.py:16
  417.7 56.2 %all-reduce.5.cloned.1.call-start = ((), (), s32[]{:S(2)}) async-start(), calls=%async_computation.1 | async-start | bytes 262144 | tf_op jit(solution)/shard_map/while/body/eval_jaxpr/psum | solution.py:28
  473.9 4.9 copy-start.1
  479.5 5.9 %collective-permute-start.1 = (f32[32,1024]{1,0:T(8,128)S(1)}, f32[32,1024]{1,0:T(8,128)S(1)}, u32[]{:S(2)}, u32[]{:S(2)}) collective-permute-start(f32[32,1024]{1,0:T(8,128)S(1)} %convolution_subtract_fusion.5), channel_id=1, source_target_pairs={{3,0},{0,1},{1,2},{2,3},{7,4},{4,5},{5,6},{6,7},{11,8},{8,9},{9,10... | collective-permute-start | bytes 393224 | tf_op jit(solution)/shard_map/while/body/eval_jaxpr/ppermute | solution.py:16
  485.4 56.2 %all-reduce.5.cloned.1.call-start = ((), (), s32[]{:S(2)}) async-start(), calls=%async_computation.1 | async-start | bytes 262144 | tf_op jit(solution)/shard_map/while/body/eval_jaxpr/psum | solution.py:28
  541.7 4.9 copy-start.1
  547.3 5.9 %collective-permute-start.1 = (f32[32,1024]{1,0:T(8,128)S(1)}, f32[32,1024]{1,0:T(8,128)S(1)}, u32[]{:S(2)}, u32[]{:S(2)}) collective-permute-start(f32[32,1024]{1,0:T(8,128)S(1)} %convolution_subtract_fusion.5), channel_id=1, source_target_pairs={{3,0},{0,1},{1,2},{2,3},{7,4},{4,5},{5,6},{6,7},{11,8},{8,9},{9,10... | collective-permute-start | bytes 393224 | tf_op jit(solution)/shard_map/while/body/eval_jaxpr/ppermute | solution.py:16
  553.2 0.8 copy-start.2
Sparse Core Ops, SparseCore 0:
  11.9 56.8 all-reduce.2
  84.0 52.3 all-reduce.2
  151.6 52.3 all-reduce.2
  218.9 52.3 all-reduce.2
  286.4 52.3 all-reduce.4
  353.8 52.3 all-reduce.4
  421.5 52.3 all-reduce.4
  489.3 52.3 all-reduce.4
where the time goes:
time: 561 us
  waiting for transfers between devices  466 us (83%)
  matrix products  66.6 us (12%)
  between operations  14 us (2%)
  starting transfers between devices  12.1 us (2%)
    psum x8, waiting for transfers between devices, refine(): projection = lax.psum(partial_value, 'rows')  431 us
    dot_general x8, matrix products, refine(): jnp.dot(projection - ridge_weight * panel_weights, inverse_gram, precisio...  39.1 us
    ppermute x8, waiting for transfers between devices, passed_along(): return lax.ppermute(block, axis, route)  35 us
    dot_general x8, matrix products, refine(): jnp.dot(panel_rows.astype(jnp.bfloat16), features, preferred_element_type...  21.7 us
    ppermute x8, starting transfers between devices, passed_along(): return lax.ppermute(block, axis, route)  12 us
  transfers between devices with their start and end apart: 16, of which 16 were waited for; matrix products, arithmetic and copies ran while one was open for 0% of the time, Pallas kernels for 0%

commit v1 on v0

v1 whole, which is shorter than its diff:
```python
import functools

import jax
import jax.numpy as jnp
from jax import lax
from jax.experimental import pallas as pl
from jax.experimental.pallas import tpu as pltpu
from jax.sharding import PartitionSpec as P

TURNS = 2
CORES = 2
TILE = 256
CHUNK = 512

ridge_weight = 0.5
MESH = pl.DeviceIdType.MESH
F32, BF16 = jnp.float32, jnp.bfloat16


def dot(a, b):
    return jnp.dot(a, b, preferred_element_type=F32)


def kernel(
    nz, nb,
    z_ref, g_ref, t_ref, w_out, r_out,
    stage, landed, gb, gs_hi, gs_lo, a_all, zt_all, res, t_stage, r_land,
    part, sums, inc_all, w_own, w_other,
    z_s, z_r, t_s, t_r, r_s, r_r, rs_s, rs_r, ag_s, ag_r, w_s, w_r, x_s, x_r,
):
    row, f = lax.axis_index("rows"), lax.axis_index("feat")
    z, c = lax.div(row, CORES), lax.rem(row, CORES)
    mate = {"rows": z * CORES + (CORES - 1 - c), "feat": f}
    ahead = {"rows": row, "feat": lax.rem(f + 1, nb)}
    behind = {"rows": row, "feat": lax.rem(f + nb - 1, nb)}
    others = [lax.rem(z + d, nz) for d in range(1, nz)]
    rl, fb = z_ref.shape
    half = t_ref.shape[1]
    fs = fb // nz
    steps = TURNS * nb
    tiles = rl // TILE
    own_chunks = rl // CHUNK
    chunks = 2 * own_chunks
    per_chunk = CHUNK // TILE

    def chip(j):
        return {"rows": j * CORES + c, "feat": f}

    def remote(src, dst, send, recv, device):
        return pltpu.make_async_remote_copy(
            src_ref=src, dst_ref=dst, send_sem=send, recv_sem=recv,
            device_id=device, device_id_type=MESH,
        )

    barrier = pltpu.get_barrier_semaphore()
    for device in [mate, ahead, behind] + [chip(j) for j in others]:
        pl.semaphore_signal(barrier, inc=1, device_id=device, device_id_type=MESH)
    pl.semaphore_wait(barrier, 3 + len(others))

    def z_copy(i):
        return remote(stage.at[i], landed.at[i], z_s.at[i], z_r.at[i], mate)

    def t_copy(q):
        return remote(t_stage.at[q], res.at[0, own_chunks + q], t_s.at[q], t_r.at[q], mate)

    for q in range(own_chunks):
        t_stage[q] = t_ref[1 - c, :, q * CHUNK:(q + 1) * CHUNK]
        t_copy(q).start()

    @pl.loop(0, tiles)
    def _(i):
        stage[i] = z_ref[pl.ds(pl.multiple_of(i * TILE, TILE), TILE), :].astype(F32)
        z_copy(i).start()

    gb[...] = g_ref[...].astype(BF16)
    g_mine = g_ref[pl.ds(pl.multiple_of(z * fs, fs), fs), :].T
    gs_hi[...] = g_mine.astype(BF16)
    gs_lo[...] = (g_mine - g_mine.astype(BF16).astype(F32)).astype(BF16)
    for q in range(own_chunks):
        res[0, q] = t_ref[c, :, q * CHUNK:(q + 1) * CHUNK]

    def prepare(tile, values):
        rows = pl.ds(pl.multiple_of(tile * TILE, TILE), TILE)
        a_all[rows, :] = dot(values.astype(BF16), gb[...]).astype(BF16)
        zt_all[tile] = values.T.astype(BF16)

    @pl.loop(0, tiles)
    def _(i):
        prepare(i, stage[i])

    @pl.loop(0, tiles)
    def _(i):
        z_copy(i).wait_recv()
        prepare(tiles + i, landed[i])

    for q in range(own_chunks):
        t_copy(q).wait_recv()

    def r_copy(s, q):
        return remote(res.at[s, q], res.at[s + 1, q], r_s.at[q], r_r.at[s + 1, q], ahead)

    def rs_copy(j):
        return remote(part.at[j], sums.at[z], rs_s.at[j], rs_r.at[z], chip(j))

    def rs_wait(j):
        remote(part.at[z], sums.at[j], rs_s.at[j], rs_r.at[j], chip(j)).wait_recv()

    def ag_copy(j):
        return remote(inc_all.at[z], inc_all.at[z], ag_s.at[j], ag_r.at[z], chip(j))

    def ag_wait(j):
        remote(inc_all.at[z], inc_all.at[j], ag_s.at[j], ag_r.at[j], chip(j)).wait_recv()

    def w_copy(panel):
        return remote(w_own.at[panel], w_other.at[panel], w_s.at[panel], w_r.at[panel], mate)

    def visit(s, turn):
        panel = lax.rem(f + steps - s, nb)
        total = jnp.zeros((half, fb), F32)
        for q in range(chunks):
            @pl.when(s > 0)
            def _():
                r_copy(s - 1, q).wait_recv()

            total += dot(res[s, q].astype(BF16), a_all[q * CHUNK:(q + 1) * CHUNK, :])
        for j in range(nz):
            part[j] = total[:, j * fs:(j + 1) * fs]
        for j in others:
            rs_copy(j).start()

        mine = part[z]
        if turn > 0:
            for j in range(nz):
                w = w_own[panel, j]
                w_hi = w.astype(BF16)
                w_lo = (w - w_hi.astype(F32)).astype(BF16)
                hi, lo = gs_hi[j * fs:(j + 1) * fs, :], gs_lo[j * fs:(j + 1) * fs, :]
                mine -= ridge_weight * (dot(w_hi, hi) + dot(w_lo, hi) + dot(w_hi, lo))
        for j in others:
            rs_wait(j)
            mine += sums[j]
        inc_all[z] = mine
        for j in others:
            ag_copy(j).start()

        fitted = [jnp.zeros((half, TILE), F32) for _ in range(2 * tiles)]
        for d, j in enumerate([z] + others):
            if d > 0:
                ag_wait(j)
            inc = inc_all[j]
            if turn > 0:
                w_own[panel, j] += inc
            else:
                w_own[panel, j] = inc
            inc = inc.astype(BF16)
            rows = pl.ds(pl.multiple_of(j * fs, fs), fs)
            for i in range(2 * tiles):
                fitted[i] += dot(inc, zt_all[i, rows, :])
        for q in range(chunks):
            @pl.when(s > 0)
            def _():
                r_copy(s - 1, q).wait_send()

            for i in range(per_chunk):
                res[s, q, :, i * TILE:(i + 1) * TILE] -= fitted[q * per_chunk + i]
            r_copy(s, q).start()
        if turn == TURNS - 1:
            w_copy(panel).start()
        for j in others:
            rs_copy(j).wait_send()
            ag_copy(j).wait_send()

    for turn in range(TURNS):
        @pl.loop(turn * nb, (turn + 1) * nb)
        def _(s, turn=turn):
            visit(s, turn)

    def x_copy(q):
        return remote(res.at[steps, own_chunks + q], r_land.at[q], x_s.at[q], x_r.at[q], mate)

    for q in range(own_chunks):
        r_copy(steps - 1, own_chunks + q).wait_recv()
        x_copy(q).start()
    for q in range(own_chunks):
        r_copy(steps - 1, q).wait_recv()
        r_out[c, :, q * CHUNK:(q + 1) * CHUNK] = res[steps, q]

    @pl.loop(0, nb)
    def _(panel):
        for j in range(nz):
            w_out[panel, c, :, j * fs:(j + 1) * fs] = w_own[panel, j]
        w_copy(panel).wait_recv()
        for j in range(nz):
            w_out[panel, 1 - c, :, j * fs:(j + 1) * fs] = w_other[panel, j]
        w_copy(panel).wait_send()

    for q in range(own_chunks):
        x_copy(q).wait_recv()
        r_out[1 - c, :, q * CHUNK:(q + 1) * CHUNK] = r_land[q]
        x_copy(q).wait_send()
        t_copy(q).wait_send()
    for q in range(chunks):
        r_copy(steps - 1, q).wait_send()

    @pl.loop(0, tiles)
    def _(i):
        z_copy(i).wait_send()


def local(features, inverse_gram, targets):
    nb = lax.axis_size("feat")
    nz = lax.axis_size("rows") // CORES
    rl, fb = features.shape
    width = targets.shape[0]
    half = width // CORES
    fs = fb // nz
    tiles, own_chunks = rl // TILE, rl // CHUNK
    chunks, steps = 2 * own_chunks, TURNS * nb
    dma = pltpu.SemaphoreType.DMA
    vmem = pl.BlockSpec(memory_space=pltpu.VMEM)
    weights, residual = pl.pallas_call(
        functools.partial(kernel, nz, nb),
        out_shape=(
            jax.ShapeDtypeStruct((nb, CORES, half, fb), F32),
            jax.ShapeDtypeStruct((CORES, half, rl), F32),
        ),
        in_specs=[vmem] * 3,
        out_specs=(vmem, vmem),
        scratch_shapes=[
            pltpu.VMEM((tiles, TILE, fb), F32),
            pltpu.VMEM((tiles, TILE, fb), F32),
            pltpu.VMEM((fb, fb), BF16),
            pltpu.VMEM((fb, fs), BF16),
            pltpu.VMEM((fb, fs), BF16),
            pltpu.VMEM((2 * rl, fb), BF16),
            pltpu.VMEM((2 * tiles, fb, TILE), BF16),
            pltpu.VMEM((steps + 1, chunks, half, CHUNK), F32),
            pltpu.VMEM((own_chunks, half, CHUNK), F32),
            pltpu.VMEM((own_chunks, half, CHUNK), F32),
            pltpu.VMEM((nz, half, fs), F32),
            pltpu.VMEM((nz, half, fs), F32),
            pltpu.VMEM((nz, half, fs), F32),
            pltpu.VMEM((nb, nz, half, fs), F32),
            pltpu.VMEM((nb, nz, half, fs), F32),
            dma((tiles,)), dma((tiles,)),
            dma((own_chunks,)), dma((own_chunks,)),
            dma((chunks,)), dma((steps + 1, chunks)),
            dma((nz,)), dma((nz,)),
            dma((nz,)), dma((nz,)),
            dma((nb,)), dma((nb,)),
            dma((own_chunks,)), dma((own_chunks,)),
        ],
        compiler_params=pltpu.CompilerParams(
            collective_id=0, has_side_effects=True, vmem_limit_bytes=50 * 2**20
        ),
    )(features, inverse_gram, targets.reshape(CORES, half, rl))
    return weights.reshape(nb * width, fb), residual.reshape(width, rl)


def solution(mesh):
    placed = (P("rows", "feat"), P("feat", None), P("feat", "rows"))
    return jax.shard_map(
        local,
        mesh=mesh,
        in_specs=placed,
        out_specs=(P(None, "feat"), P("feat", "rows")),
        check_vma=False,
    )
```

time: 561 us -> 123 us (0.22)
  waiting for transfers between devices: 466 us -> 0 us
  Pallas kernels: 0 us -> 118 us
  matrix products: 66.6 us -> 0 us
  between operations: 14 us -> 0.65 us
  starting transfers between devices: 12.1 us -> 0 us
    psum x8 -> x0, waiting for transfers between devices: 431 us -> none  [refine(): projection = lax.psum(partial_value, 'rows')]
    pallas_call x0 -> x1, Pallas kernels: none -> 118 us  [local(): pl.pallas_call(functools.partial(kernel, nz, nb), out_shape=(jax.ShapeDty...]
    dot_general x24 -> x0, matrix products: 66.6 us -> none  [the longest x8 39.1 us: refine(): jnp.dot(projection - ridge_weight * panel_weights, inverse_gram, precisio...]
    ppermute x8 -> x0, waiting for transfers between devices: 35 us -> none  [passed_along(): return lax.ppermute(block, axis, route)]
    ppermute x8 -> x0, starting transfers between devices: 12 us -> none  [passed_along(): return lax.ppermute(block, axis, route)]
  transfers between devices with their start and end apart: 16 -> 0, of which waited for: 16 -> 0; matrix products, arithmetic and copies ran while one was open for 0% -> 0% of each run, Pallas kernels for 0% -> 0%
where the time goes in v1:
time: 123 us
  Pallas kernels  118 us (96%)
  local copies, waits for them, and re-layouts  3.94 us (3%)
    pallas_call x1, Pallas kernels, local(): pl.pallas_call(functools.partial(kernel, nz, nb), out_shape=(jax.ShapeDty...  118 us
    unnamed x6, local copies, waits for them, and re-layouts  3.94 us

profile of v1, /device:TPU:0, one launch (start us, length us, event | category | flops | bytes accessed | tf_op | source)
XLA Modules:
  0.0 122.7 jit_solution(18242481116663408515)
XLA Ops:
  0.6 0.0 copy-start
  0.6 1.6 %copy-done = bf16[1024,1024]{1,0:T(8,128)(2,1)S(1)} copy-done((bf16[1024,1024]{1,0:T(8,128)(2,1)S(1)}, bf16[1024,1024]{1,0:T(8,128)(2,1)}, u32[]{:S(2)}) %copy-start) | copy-done | bytes 2097176
  2.2 0.0 copy-start.1
  2.2 0.9 copy-done.1
  3.1 118.1 %shard_map.50 = (f32[4,2,16,1024]{3,2,1,0:T(8,128)S(1)}, f32[2,16,1024]{2,1,0:T(8,128)S(1)}) custom-call(bf16[1024,1024]{1,0:T(8,128)(2,1)S(1)} %copy-done, f32[1024,1024]{1,0:T(8,128)} %g_ref.1, f32[2,16,1024]{2,1,0:T(8,128)S(1)} %bitcast.4), custom_call_target="tpu_custom_call" | custom-call | tf_op jit(solution)/shard_map/pallas_call | solution.py:221
  121.2 0.8 copy.7
  122.0 0.7 copy.8
Async XLA Ops:
  0.6 1.6 %copy-start = (bf16[1024,1024]{1,0:T(8,128)(2,1)S(1)}, bf16[1024,1024]{1,0:T(8,128)(2,1)}, u32[]{:S(2)}) copy-start(bf16[1024,1024]{1,0:T(8,128)(2,1)} %z_ref.1) | copy-start | bytes 6291460
  2.2 0.9 copy-start.1

commit v2 on v1

v2 whole, which is shorter than its diff:
```python
import functools

import jax
import jax.numpy as jnp
from jax import lax
from jax.experimental import pallas as pl
from jax.experimental.pallas import tpu as pltpu
from jax.sharding import PartitionSpec as P

TURNS = 2
CORES = 2
TILE = 256
PARTS = 2
CHUNK = 512

ridge_weight = 0.5
MESH = pl.DeviceIdType.MESH
F32, BF16 = jnp.float32, jnp.bfloat16


def dot(a, b):
    return jnp.dot(a, b, preferred_element_type=F32)


def kernel(
    nz, nb,
    z_ref, g_ref, t_ref, w_out, r_out,
    stage, landed, gb, gs_hi, gs_lo, a_all, zt_all, res, t_stage, r_land,
    part, sums, inc_all, w_own, w_other,
    z_s, z_r, t_s, t_r, r_s, r_r, rs_s, rs_r, ag_s, ag_r, w_s, w_r, x_s, x_r,
):
    row, f = lax.axis_index("rows"), lax.axis_index("feat")
    z, c = lax.div(row, CORES), lax.rem(row, CORES)
    mate = {"rows": z * CORES + (CORES - 1 - c), "feat": f}
    ahead = {"rows": row, "feat": lax.rem(f + 1, nb)}
    behind = {"rows": row, "feat": lax.rem(f + nb - 1, nb)}
    others = [lax.rem(z + d, nz) for d in range(1, nz)]
    rl, fb = z_ref.shape
    half = t_ref.shape[2]
    fs = fb // nz
    steps = TURNS * nb
    tiles = rl // TILE
    own_chunks = rl // CHUNK
    chunks = 2 * own_chunks
    per_chunk = CHUNK // TILE

    def chip(j):
        return {"rows": j * CORES + c, "feat": f}

    def remote(src, dst, send, recv, device):
        return pltpu.make_async_remote_copy(
            src_ref=src, dst_ref=dst, send_sem=send, recv_sem=recv,
            device_id=device, device_id_type=MESH,
        )

    barrier = pltpu.get_barrier_semaphore()
    for device in [mate, ahead, behind] + [chip(j) for j in others]:
        pl.semaphore_signal(barrier, inc=1, device_id=device, device_id_type=MESH)
    pl.semaphore_wait(barrier, 3 + len(others))

    def z_copy(i):
        return remote(stage.at[i], landed.at[i], z_s.at[i], z_r.at[i], mate)

    both = [(x, q) for x in range(PARTS) for q in range(own_chunks)]

    def t_copy(x, q):
        return remote(
            t_stage.at[x, q], res.at[0, x, own_chunks + q], t_s.at[x, q], t_r.at[x, q], mate
        )

    for x, q in both:
        t_stage[x, q] = t_ref[1 - c, x, :, q * CHUNK:(q + 1) * CHUNK]
        t_copy(x, q).start()

    @pl.loop(0, tiles)
    def _(i):
        stage[i] = z_ref[pl.ds(pl.multiple_of(i * TILE, TILE), TILE), :].astype(F32)
        z_copy(i).start()

    gb[...] = g_ref[...].astype(BF16)
    g_mine = g_ref[pl.ds(pl.multiple_of(z * fs, fs), fs), :].T
    gs_hi[...] = g_mine.astype(BF16)
    gs_lo[...] = (g_mine - g_mine.astype(BF16).astype(F32)).astype(BF16)
    for x, q in both:
        res[0, x, q] = t_ref[c, x, :, q * CHUNK:(q + 1) * CHUNK]
    w_own[...] = jnp.zeros_like(w_own)

    def prepare(tile, values):
        rows = pl.ds(pl.multiple_of(tile * TILE, TILE), TILE)
        a_all[rows, :] = dot(values.astype(BF16), gb[...]).astype(BF16)
        zt_all[tile] = values.T.astype(BF16)

    @pl.loop(0, tiles)
    def _(i):
        prepare(i, stage[i])

    @pl.loop(0, tiles)
    def _(i):
        z_copy(i).wait_recv()
        prepare(tiles + i, landed[i])

    for x, q in both:
        t_copy(x, q).wait_recv()

    def r_copy(x, s, q):
        return remote(
            res.at[s, x, q], res.at[s + 1, x, q], r_s.at[x, q], r_r.at[s + 1, x, q], ahead
        )

    def rs_copy(x, j):
        return remote(part.at[x, j], sums.at[x, z], rs_s.at[x, j], rs_r.at[x, z], chip(j))

    def rs_wait(x, j):
        remote(part.at[x, z], sums.at[x, j], rs_s.at[x, j], rs_r.at[x, j], chip(j)).wait_recv()

    def ag_copy(x, j):
        return remote(inc_all.at[x, z], inc_all.at[x, z], ag_s.at[x, j], ag_r.at[x, z], chip(j))

    def ag_wait(x, j):
        remote(inc_all.at[x, z], inc_all.at[x, j], ag_s.at[x, j], ag_r.at[x, j], chip(j)).wait_recv()

    def w_copy(x, panel):
        return remote(
            w_own.at[panel, x], w_other.at[panel, x], w_s.at[panel, x], w_r.at[panel, x], mate
        )

    def panel_at(s):
        return lax.rem(f + steps - s, nb)

    def project(x, s):
        total = jnp.zeros((half, fb), F32)
        for q in range(chunks):
            @pl.when(s > 0)
            def _():
                r_copy(x, s - 1, q).wait_recv()

            total += dot(res[s, x, q].astype(BF16), a_all[q * CHUNK:(q + 1) * CHUNK, :])
        for j in range(nz):
            part[x, j] = total[:, j * fs:(j + 1) * fs]
        for j in others:
            rs_copy(x, j).start()

    def add_up(x, s):
        panel = panel_at(s)

        @pl.when(s >= nb)
        def _():
            pull = jnp.zeros((half, fs), F32)
            for j in range(nz):
                w = w_own[panel, x, j]
                w_hi = w.astype(BF16)
                w_lo = (w - w_hi.astype(F32)).astype(BF16)
                hi, lo = gs_hi[j * fs:(j + 1) * fs, :], gs_lo[j * fs:(j + 1) * fs, :]
                pull += dot(w_hi, hi) + dot(w_lo, hi) + dot(w_hi, lo)
            part[x, z] -= ridge_weight * pull

        mine = part[x, z]
        for j in others:
            rs_wait(x, j)
            mine += sums[x, j]
        inc_all[x, z] = mine
        for j in others:
            ag_copy(x, j).start()

    def update(x, s):
        panel = panel_at(s)
        fitted = [jnp.zeros((half, TILE), F32) for _ in range(2 * tiles)]
        for d, j in enumerate([z] + others):
            if d > 0:
                ag_wait(x, j)
            inc = inc_all[x, j]
            w_own[panel, x, j] += inc
            inc = inc.astype(BF16)
            rows = pl.ds(pl.multiple_of(j * fs, fs), fs)
            for i in range(2 * tiles):
                fitted[i] += dot(inc, zt_all[i, rows, :])
        for q in range(chunks):
            @pl.when(s > 0)
            def _():
                r_copy(x, s - 1, q).wait_send()

            for i in range(per_chunk):
                res[s, x, q, :, i * TILE:(i + 1) * TILE] -= fitted[q * per_chunk + i]
            r_copy(x, s, q).start()

        @pl.when(s >= steps - nb)
        def _():
            w_copy(x, panel).start()

        for j in others:
            rs_copy(x, j).wait_send()
            ag_copy(x, j).wait_send()

    @pl.loop(0, steps)
    def _(s):
        project(0, s)

        @pl.when(s > 0)
        def _():
            update(1, s - 1)

        add_up(0, s)
        project(1, s)
        update(0, s)
        add_up(1, s)

    update(1, steps - 1)

    def x_copy(x, q):
        return remote(
            res.at[steps, x, own_chunks + q], r_land.at[x, q], x_s.at[x, q], x_r.at[x, q], mate
        )

    for x, q in both:
        r_copy(x, steps - 1, own_chunks + q).wait_recv()
        x_copy(x, q).start()
    for x, q in both:
        r_copy(x, steps - 1, q).wait_recv()
        r_out[c, x, :, q * CHUNK:(q + 1) * CHUNK] = res[steps, x, q]

    @pl.loop(0, nb)
    def _(panel):
        for x in range(PARTS):
            for j in range(nz):
                w_out[panel, c, x, :, j * fs:(j + 1) * fs] = w_own[panel, x, j]
            w_copy(x, panel).wait_recv()
            for j in range(nz):
                w_out[panel, 1 - c, x, :, j * fs:(j + 1) * fs] = w_other[panel, x, j]
            w_copy(x, panel).wait_send()

    for x, q in both:
        x_copy(x, q).wait_recv()
        r_out[1 - c, x, :, q * CHUNK:(q + 1) * CHUNK] = r_land[x, q]
        x_copy(x, q).wait_send()
        t_copy(x, q).wait_send()
    for x in range(PARTS):
        for q in range(chunks):
            r_copy(x, steps - 1, q).wait_send()

    @pl.loop(0, tiles)
    def _(i):
        z_copy(i).wait_send()


def local(features, inverse_gram, targets):
    nb = lax.axis_size("feat")
    nz = lax.axis_size("rows") // CORES
    rl, fb = features.shape
    width = targets.shape[0]
    half = width // (CORES * PARTS)
    fs = fb // nz
    tiles, own_chunks = rl // TILE, rl // CHUNK
    chunks, steps = 2 * own_chunks, TURNS * nb
    dma = pltpu.SemaphoreType.DMA
    vmem = pl.BlockSpec(memory_space=pltpu.VMEM)
    weights, residual = pl.pallas_call(
        functools.partial(kernel, nz, nb),
        out_shape=(
            jax.ShapeDtypeStruct((nb, CORES, PARTS, half, fb), F32),
            jax.ShapeDtypeStruct((CORES, PARTS, half, rl), F32),
        ),
        in_specs=[vmem] * 3,
        out_specs=(vmem, vmem),
        scratch_shapes=[
            pltpu.VMEM((tiles, TILE, fb), F32),
            pltpu.VMEM((tiles, TILE, fb), F32),
            pltpu.VMEM((fb, fb), BF16),
            pltpu.VMEM((fb, fs), BF16),
            pltpu.VMEM((fb, fs), BF16),
            pltpu.VMEM((2 * rl, fb), BF16),
            pltpu.VMEM((2 * tiles, fb, TILE), BF16),
            pltpu.VMEM((steps + 1, PARTS, chunks, half, CHUNK), F32),
            pltpu.VMEM((PARTS, own_chunks, half, CHUNK), F32),
            pltpu.VMEM((PARTS, own_chunks, half, CHUNK), F32),
            pltpu.VMEM((PARTS, nz, half, fs), F32),
            pltpu.VMEM((PARTS, nz, half, fs), F32),
            pltpu.VMEM((PARTS, nz, half, fs), F32),
            pltpu.VMEM((nb, PARTS, nz, half, fs), F32),
            pltpu.VMEM((nb, PARTS, nz, half, fs), F32),
            dma((tiles,)), dma((tiles,)),
            dma((PARTS, own_chunks)), dma((PARTS, own_chunks)),
            dma((PARTS, chunks)), dma((steps + 1, PARTS, chunks)),
            dma((PARTS, nz)), dma((PARTS, nz)),
            dma((PARTS, nz)), dma((PARTS, nz)),
            dma((nb, PARTS)), dma((nb, PARTS)),
            dma((PARTS, own_chunks)), dma((PARTS, own_chunks)),
        ],
        compiler_params=pltpu.CompilerParams(
            collective_id=0, has_side_effects=True, vmem_limit_bytes=50 * 2**20
        ),
    )(features, inverse_gram, targets.reshape(CORES, PARTS, half, rl))
    return weights.reshape(nb * width, fb), residual.reshape(width, rl)


def solution(mesh):
    placed = (P("rows", "feat"), P("feat", None), P("feat", "rows"))
    return jax.shard_map(
        local,
        mesh=mesh,
        in_specs=placed,
        out_specs=(P(None, "feat"), P("feat", "rows")),
        check_vma=False,
    )
```

time: 123 us -> 121 us (0.984)
  Pallas kernels: 118 us -> 116 us
    pallas_call x1, Pallas kernels: 118 us -> 116 us  [local(): pl.pallas_call(functools.partial(kernel, nz, nb), out_shape=(jax.ShapeDty...]
where the time goes in v2:
time: 121 us
  Pallas kernels  116 us (96%)
  local copies, waits for them, and re-layouts  3.94 us (3%)
    pallas_call x1, Pallas kernels, local(): pl.pallas_call(functools.partial(kernel, nz, nb), out_shape=(jax.ShapeDty...  116 us
    unnamed x6, local copies, waits for them, and re-layouts  3.94 us

profile of v2, /device:TPU:0, one launch (start us, length us, event | category | flops | bytes accessed | tf_op | source)
XLA Modules:
  0.0 120.6 jit_solution(11094697993949049854)
XLA Ops:
  0.6 0.0 copy-start
  0.6 1.6 %copy-done = bf16[1024,1024]{1,0:T(8,128)(2,1)S(1)} copy-done((bf16[1024,1024]{1,0:T(8,128)(2,1)S(1)}, bf16[1024,1024]{1,0:T(8,128)(2,1)}, u32[]{:S(2)}) %copy-start) | copy-done | bytes 2097176
  2.2 0.0 copy-start.1
  2.2 0.9 copy-done.1
  3.1 116.0 %shard_map.50 = (f32[4,2,2,8,1024]{4,3,2,1,0:T(8,128)S(1)}, f32[2,2,8,1024]{3,2,1,0:T(8,128)S(1)}) custom-call(bf16[1024,1024]{1,0:T(8,128)(2,1)S(1)} %copy-done, f32[1024,1024]{1,0:T(8,128)} %g_ref.1, f32[2,2,8,1024]{3,2,1,0:T(8,128)S(1)} %bitcast.4), custom_call_target="tpu_custom_call" | custom-call | tf_op jit(solution)/shard_map/pallas_call | solution.py:256
  119.1 0.8 copy.7
  119.9 0.7 copy.8
Async XLA Ops:
  0.6 1.6 %copy-start = (bf16[1024,1024]{1,0:T(8,128)(2,1)S(1)}, bf16[1024,1024]{1,0:T(8,128)(2,1)}, u32[]{:S(2)}) copy-start(bf16[1024,1024]{1,0:T(8,128)(2,1)} %z_ref.1) | copy-start | bytes 6291460
  2.2 0.9 copy-start.1

commit v3 on v2

--- a/solution.py
+++ b/solution.py
@@ -24,10 +24,10 @@
 
 def kernel(
     nz, nb,
-    z_ref, g_ref, t_ref, w_out, r_out,
-    stage, landed, gb, gs_hi, gs_lo, a_all, zt_all, res, t_stage, r_land,
+    z_hbm, g_hbm, t_ref, t_flat, w_out, r_out,
+    z_own, g_ref, p_first, p_land, stage, landed, gb, gs_hi, gs_lo, a_all, zt_all, res, t_stage,
     part, sums, inc_all, w_own, w_other,
-    z_s, z_r, t_s, t_r, r_s, r_r, rs_s, rs_r, ag_s, ag_r, w_s, w_r, x_s, x_r,
+    z_s, z_r, t_s, t_r, r_s, r_r, rs_s, rs_r, ag_s, ag_r, w_s, w_r, in_s, p_s, p_r,
 ):
     row, f = lax.axis_index("rows"), lax.axis_index("feat")
     z, c = lax.div(row, CORES), lax.rem(row, CORES)
@@ -35,7 +35,9 @@
     ahead = {"rows": row, "feat": lax.rem(f + 1, nb)}
     behind = {"rows": row, "feat": lax.rem(f + nb - 1, nb)}
     others = [lax.rem(z + d, nz) for d in range(1, nz)]
-    rl, fb = z_ref.shape
+    mate_ahead = {"rows": mate["rows"], "feat": ahead["feat"]}
+    mate_behind = {"rows": mate["rows"], "feat": behind["feat"]}
+    rl, fb = z_hbm.shape
     half = t_ref.shape[2]
     fs = fb // nz
     steps = TURNS * nb
@@ -53,10 +55,22 @@
             device_id=device, device_id_type=MESH,
         )
 
+    def load_z(i):
+        rows = pl.ds(pl.multiple_of(i * TILE, TILE), TILE)
+        return pltpu.make_async_copy(z_hbm.at[rows, :], z_own.at[i], in_s.at[i])
+
+    load_g = pltpu.make_async_copy(g_hbm, g_ref, in_s.at[tiles])
+
+    @pl.loop(0, tiles)
+    def _(i):
+        load_z(i).start()
+
+    load_g.start()
+
     barrier = pltpu.get_barrier_semaphore()
-    for device in [mate, ahead, behind] + [chip(j) for j in others]:
+    for device in [mate, ahead, behind, mate_ahead, mate_behind] + [chip(j) for j in others]:
         pl.semaphore_signal(barrier, inc=1, device_id=device, device_id_type=MESH)
-    pl.semaphore_wait(barrier, 3 + len(others))
+    pl.semaphore_wait(barrier, 5 + len(others))
 
     def z_copy(i):
         return remote(stage.at[i], landed.at[i], z_s.at[i], z_r.at[i], mate)
@@ -74,9 +88,11 @@
 
     @pl.loop(0, tiles)
     def _(i):
-        stage[i] = z_ref[pl.ds(pl.multiple_of(i * TILE, TILE), TILE), :].astype(F32)
+        load_z(i).wait()
+        stage[i] = z_own[i].astype(F32)
         z_copy(i).start()
 
+    load_g.wait()
     gb[...] = g_ref[...].astype(BF16)
     g_mine = g_ref[pl.ds(pl.multiple_of(z * fs, fs), fs), :].T
     gs_hi[...] = g_mine.astype(BF16)
@@ -92,19 +108,14 @@
 
     @pl.loop(0, tiles)
     def _(i):
-        prepare(i, stage[i])
-
-    @pl.loop(0, tiles)
-    def _(i):
-        z_copy(i).wait_recv()
-        prepare(tiles + i, landed[i])
-
-    for x, q in both:
-        t_copy(x, q).wait_recv()
+        rows = pl.ds(pl.multiple_of(i * TILE, TILE), TILE)
+        a_all[rows, :] = dot(z_own[i], gb[...]).astype(BF16)
 
     def r_copy(x, s, q):
+        home = lax.div(s, steps - 1) * (q // own_chunks)
+        device = {"rows": row + home * (mate["rows"] - row), "feat": ahead["feat"]}
         return remote(
-            res.at[s, x, q], res.at[s + 1, x, q], r_s.at[x, q], r_r.at[s + 1, x, q], ahead
+            res.at[s, x, q], res.at[s + 1, x, q], r_s.at[x, q], r_r.at[s + 1, x, q], device
         )
 
     def rs_copy(x, j):
@@ -127,18 +138,18 @@
     def panel_at(s):
         return lax.rem(f + steps - s, nb)
 
-    def project(x, s):
-        total = jnp.zeros((half, fb), F32)
-        for q in range(chunks):
-            @pl.when(s > 0)
-            def _():
-                r_copy(x, s - 1, q).wait_recv()
-
-            total += dot(res[s, x, q].astype(BF16), a_all[q * CHUNK:(q + 1) * CHUNK, :])
+    def send_parts(x, total):
         for j in range(nz):
             part[x, j] = total[:, j * fs:(j + 1) * fs]
         for j in others:
             rs_copy(x, j).start()
+
+    def project(x, s):
+        total = jnp.zeros((half, fb), F32)
+        for q in range(chunks):
+            r_copy(x, s - 1, q).wait_recv()
+            total += dot(res[s, x, q].astype(BF16), a_all[q * CHUNK:(q + 1) * CHUNK, :])
+        send_parts(x, total)
 
     def add_up(x, s):
         panel = panel_at(s)
@@ -191,14 +202,42 @@
             rs_copy(x, j).wait_send()
             ag_copy(x, j).wait_send()
 
-    @pl.loop(0, steps)
+    total = dot(t_flat[...].astype(BF16), a_all[:rl, :])
+    for h in range(CORES):
+        for x in range(PARTS):
+            first = (h * PARTS + x) * half
+            p_first[h, x] = total[first:first + half, :]
+    p_copy = remote(p_first.at[1 - c], p_land, p_s, p_r, mate)
+    p_copy.start()
+
+    @pl.loop(0, tiles // 2)
+    def _(i):
+        zt_all[i] = stage[i].T.astype(BF16)
+
+    p_copy.wait_recv()
+    for x in range(PARTS):
+        send_parts(x, p_first[c, x] + p_land[x])
+
+    @pl.loop(tiles // 2, tiles)
+    def _(i):
+        zt_all[i] = stage[i].T.astype(BF16)
+
+    add_up(0, 0)
+    add_up(1, 0)
+
+    @pl.loop(0, tiles)
+    def _(i):
+        z_copy(i).wait_recv()
+        prepare(tiles + i, landed[i])
+
+    for x, q in both:
+        t_copy(x, q).wait_recv()
+    update(0, 0)
+
+    @pl.loop(1, steps)
     def _(s):
         project(0, s)
-
-        @pl.when(s > 0)
-        def _():
-            update(1, s - 1)
-
+        update(1, s - 1)
         add_up(0, s)
         project(1, s)
         update(0, s)
@@ -206,17 +245,10 @@
 
     update(1, steps - 1)
 
-    def x_copy(x, q):
-        return remote(
-            res.at[steps, x, own_chunks + q], r_land.at[x, q], x_s.at[x, q], x_r.at[x, q], mate
-        )
-
-    for x, q in both:
-        r_copy(x, steps - 1, own_chunks + q).wait_recv()
-        x_copy(x, q).start()
-    for x, q in both:
-        r_copy(x, steps - 1, q).wait_recv()
-        r_out[c, x, :, q * CHUNK:(q + 1) * CHUNK] = res[steps, x, q]
+    for x, q in both:
+        for h, k in ((c, q), (1 - c, own_chunks + q)):
+            r_copy(x, steps - 1, k).wait_recv()
+            r_out[h, x, :, q * CHUNK:(q + 1) * CHUNK] = res[steps, x, k]
 
     @pl.loop(0, nb)
     def _(panel):
@@ -228,10 +260,8 @@
                 w_out[panel, 1 - c, x, :, j * fs:(j + 1) * fs] = w_other[panel, x, j]
             w_copy(x, panel).wait_send()
 
-    for x, q in both:
-        x_copy(x, q).wait_recv()
-        r_out[1 - c, x, :, q * CHUNK:(q + 1) * CHUNK] = r_land[x, q]
-        x_copy(x, q).wait_send()
+    p_copy.wait_send()
+    for x, q in both:
         t_copy(x, q).wait_send()
     for x in range(PARTS):
         for q in range(chunks):
@@ -252,6 +282,7 @@
     tiles, own_chunks = rl // TILE, rl // CHUNK
     chunks, steps = 2 * own_chunks, TURNS * nb
     dma = pltpu.SemaphoreType.DMA
+    hbm = pl.BlockSpec(memory_space=pl.ANY)
     vmem = pl.BlockSpec(memory_space=pltpu.VMEM)
     weights, residual = pl.pallas_call(
         functools.partial(kernel, nz, nb),
@@ -259,9 +290,13 @@
             jax.ShapeDtypeStruct((nb, CORES, PARTS, half, fb), F32),
             jax.ShapeDtypeStruct((CORES, PARTS, half, rl), F32),
         ),
-        in_specs=[vmem] * 3,
+        in_specs=[hbm, hbm, vmem, vmem],
         out_specs=(vmem, vmem),
         scratch_shapes=[
+            pltpu.VMEM((tiles, TILE, fb), BF16),
+            pltpu.VMEM((fb, fb), F32),
+            pltpu.VMEM((CORES, PARTS, half, fb), F32),
+            pltpu.VMEM((PARTS, half, fb), F32),
             pltpu.VMEM((tiles, TILE, fb), F32),
             pltpu.VMEM((tiles, TILE, fb), F32),
             pltpu.VMEM((fb, fb), BF16),
@@ -270,7 +305,6 @@
             pltpu.VMEM((2 * rl, fb), BF16),
             pltpu.VMEM((2 * tiles, fb, TILE), BF16),
             pltpu.VMEM((steps + 1, PARTS, chunks, half, CHUNK), F32),
-            pltpu.VMEM((PARTS, own_chunks, half, CHUNK), F32),
             pltpu.VMEM((PARTS, own_chunks, half, CHUNK), F32),
             pltpu.VMEM((PARTS, nz, half, fs), F32),
             pltpu.VMEM((PARTS, nz, half, fs), F32),
@@ -283,12 +317,12 @@
             dma((PARTS, nz)), dma((PARTS, nz)),
             dma((PARTS, nz)), dma((PARTS, nz)),
             dma((nb, PARTS)), dma((nb, PARTS)),
-            dma((PARTS, own_chunks)), dma((PARTS, own_chunks)),
+            dma((tiles + 1,)), dma, dma,
         ],
         compiler_params=pltpu.CompilerParams(
             collective_id=0, has_side_effects=True, vmem_limit_bytes=50 * 2**20
         ),
-    )(features, inverse_gram, targets.reshape(CORES, PARTS, half, rl))
+    )(features, inverse_gram, targets.reshape(CORES, PARTS, half, rl), targets)
     return weights.reshape(nb * width, fb), residual.reshape(width, rl)
 
 

time: 121 us -> 117 us (0.967)
  Pallas kernels: 116 us -> 113 us
    pallas_call x1, Pallas kernels: 116 us -> 113 us  [local(): pl.pallas_call(functools.partial(kernel, nz, nb), out_shape=(jax.ShapeDty...]
where the time goes in v3:
time: 117 us
  Pallas kernels  113 us (97%)
  local copies, waits for them, and re-layouts  3.94 us (3%)
    pallas_call x1, Pallas kernels, local(): pl.pallas_call(functools.partial(kernel, nz, nb), out_shape=(jax.ShapeDty...  113 us
    unnamed x6, local copies, waits for them, and re-layouts  3.94 us

profile of v3, /device:TPU:0, one launch (start us, length us, event | category | flops | bytes accessed | tf_op | source)
XLA Modules:
  0.0 117.2 jit_solution(10548413494102129674)
XLA Ops:
  0.6 0.0 copy-start
  0.6 1.6 %copy-done = bf16[1024,1024]{1,0:T(8,128)(2,1)S(1)} copy-done((bf16[1024,1024]{1,0:T(8,128)(2,1)S(1)}, bf16[1024,1024]{1,0:T(8,128)(2,1)}, u32[]{:S(2)}) %copy-start) | copy-done | bytes 2097176
  2.2 0.0 copy-start.1
  2.2 0.9 copy-done.1
  3.1 112.6 %shard_map.50 = (f32[4,2,2,8,1024]{4,3,2,1,0:T(8,128)S(1)}, f32[2,2,8,1024]{3,2,1,0:T(8,128)S(1)}) custom-call(bf16[1024,1024]{1,0:T(8,128)(2,1)S(1)} %copy-done, f32[1024,1024]{1,0:T(8,128)} %g_hbm.1, f32[2,2,8,1024]{3,2,1,0:T(8,128)S(1)} %bitcast.3, f32[32,1024]{1,0:T(8,128)S(1)} %copy-done.1), custom_call_target="tpu_custom_call" | custom-call | tf_op jit(solution)/shard_map/pallas_call | solution.py:287
  115.8 0.8 copy.7
  116.6 0.7 copy.8
Async XLA Ops:
  0.6 1.6 %copy-start = (bf16[1024,1024]{1,0:T(8,128)(2,1)S(1)}, bf16[1024,1024]{1,0:T(8,128)(2,1)}, u32[]{:S(2)}) copy-start(bf16[1024,1024]{1,0:T(8,128)(2,1)} %z_hbm.1) | copy-start | bytes 6291460
  2.2 0.9 copy-start.1

commit v4 on v3

--- a/solution.py
+++ b/solution.py
@@ -10,6 +10,7 @@
 TURNS = 2
 CORES = 2
 TILE = 256
+PIECES = 2
 PARTS = 2
 CHUNK = 512
 
@@ -26,8 +27,8 @@
     nz, nb,
     z_hbm, g_hbm, t_ref, t_flat, w_out, r_out,
     z_own, g_ref, p_first, p_land, stage, landed, gb, gs_hi, gs_lo, a_all, zt_all, res, t_stage,
-    part, sums, inc_all, w_own, w_other,
-    z_s, z_r, t_s, t_r, r_s, r_r, rs_s, rs_r, ag_s, ag_r, w_s, w_r, in_s, p_s, p_r,
+    pull, sums, w_own, w_other,
+    z_s, z_r, t_s, t_r, r_s, r_r, sum_s, sum_r, w_s, w_r, in_s, p_s, p_r,
 ):
     row, f = lax.axis_index("rows"), lax.axis_index("feat")
     z, c = lax.div(row, CORES), lax.rem(row, CORES)
@@ -39,7 +40,7 @@
     mate_behind = {"rows": mate["rows"], "feat": behind["feat"]}
     rl, fb = z_hbm.shape
     half = t_ref.shape[2]
-    fs = fb // nz
+    fs, fp = fb // nz, fb // PIECES
     steps = TURNS * nb
     tiles = rl // TILE
     own_chunks = rl // CHUNK
@@ -94,12 +95,13 @@
 
     load_g.wait()
     gb[...] = g_ref[...].astype(BF16)
-    g_mine = g_ref[pl.ds(pl.multiple_of(z * fs, fs), fs), :].T
+    g_mine = g_ref[pl.ds(pl.multiple_of(z * fs, fs), fs), :]
     gs_hi[...] = g_mine.astype(BF16)
     gs_lo[...] = (g_mine - g_mine.astype(BF16).astype(F32)).astype(BF16)
     for x, q in both:
         res[0, x, q] = t_ref[c, x, :, q * CHUNK:(q + 1) * CHUNK]
     w_own[...] = jnp.zeros_like(w_own)
+    pull[...] = jnp.zeros_like(pull)
 
     def prepare(tile, values):
         rows = pl.ds(pl.multiple_of(tile * TILE, TILE), TILE)
@@ -118,17 +120,15 @@
             res.at[s, x, q], res.at[s + 1, x, q], r_s.at[x, q], r_r.at[s + 1, x, q], device
         )
 
-    def rs_copy(x, j):
-        return remote(part.at[x, j], sums.at[x, z], rs_s.at[x, j], rs_r.at[x, z], chip(j))
-
-    def rs_wait(x, j):
-        remote(part.at[x, z], sums.at[x, j], rs_s.at[x, j], rs_r.at[x, j], chip(j)).wait_recv()
-
-    def ag_copy(x, j):
-        return remote(inc_all.at[x, z], inc_all.at[x, z], ag_s.at[x, j], ag_r.at[x, z], chip(j))
-
-    def ag_wait(x, j):
-        remote(inc_all.at[x, z], inc_all.at[x, j], ag_s.at[x, j], ag_r.at[x, j], chip(j)).wait_recv()
+    def sum_copy(x, s, j, k):
+        slot = lax.rem(s, 2)
+        own = sums.at[slot, x, z, k]
+        return remote(own, own, sum_s.at[x, j, k], sum_r.at[slot, x, z, k], chip(j))
+
+    def sum_wait(x, s, j, k):
+        slot = lax.rem(s, 2)
+        theirs = sums.at[slot, x, j, k]
+        remote(theirs, theirs, sum_s.at[x, j, k], sum_r.at[slot, x, j, k], chip(j)).wait_recv()
 
     def w_copy(x, panel):
         return remote(
@@ -138,53 +138,43 @@
     def panel_at(s):
         return lax.rem(f + steps - s, nb)
 
-    def send_parts(x, total):
-        for j in range(nz):
-            part[x, j] = total[:, j * fs:(j + 1) * fs]
-        for j in others:
-            rs_copy(x, j).start()
+    def send_parts(x, s, total):
+        for k in range(PIECES):
+            sums[lax.rem(s, 2), x, z, k] = total[:, k * fp:(k + 1) * fp]
+            for j in others:
+                sum_copy(x, s, j, k).start()
 
     def project(x, s):
-        total = jnp.zeros((half, fb), F32)
+        panel = panel_at(s)
+
+        @pl.when(s >= nb)
+        def _():
+            w = w_own[panel, x, z]
+            w_hi = w.astype(BF16)
+            w_lo = (w - w_hi.astype(F32)).astype(BF16)
+            hi, lo = gs_hi[...], gs_lo[...]
+            pull[x] = ridge_weight * (dot(w_hi, hi) + dot(w_lo, hi) + dot(w_hi, lo))
+
+        total = -pull[x]
         for q in range(chunks):
             r_copy(x, s - 1, q).wait_recv()
             total += dot(res[s, x, q].astype(BF16), a_all[q * CHUNK:(q + 1) * CHUNK, :])
-        send_parts(x, total)
-
-    def add_up(x, s):
-        panel = panel_at(s)
-
-        @pl.when(s >= nb)
-        def _():
-            pull = jnp.zeros((half, fs), F32)
-            for j in range(nz):
-                w = w_own[panel, x, j]
-                w_hi = w.astype(BF16)
-                w_lo = (w - w_hi.astype(F32)).astype(BF16)
-                hi, lo = gs_hi[j * fs:(j + 1) * fs, :], gs_lo[j * fs:(j + 1) * fs, :]
-                pull += dot(w_hi, hi) + dot(w_lo, hi) + dot(w_hi, lo)
-            part[x, z] -= ridge_weight * pull
-
-        mine = part[x, z]
-        for j in others:
-            rs_wait(x, j)
-            mine += sums[x, j]
-        inc_all[x, z] = mine
-        for j in others:
-            ag_copy(x, j).start()
+        send_parts(x, s, total)
 
     def update(x, s):
         panel = panel_at(s)
         fitted = [jnp.zeros((half, TILE), F32) for _ in range(2 * tiles)]
-        for d, j in enumerate([z] + others):
-            if d > 0:
-                ag_wait(x, j)
-            inc = inc_all[x, j]
-            w_own[panel, x, j] += inc
+        for k in range(PIECES):
+            for j in others:
+                sum_wait(x, s, j, k)
+            inc = sums[lax.rem(s, 2), x, 0, k]
+            for j in range(1, nz):
+                inc += sums[lax.rem(s, 2), x, j, k]
+            for j in range(fp // fs):
+                w_own[panel, x, k * (fp // fs) + j] += inc[:, j * fs:(j + 1) * fs]
             inc = inc.astype(BF16)
-            rows = pl.ds(pl.multiple_of(j * fs, fs), fs)
             for i in range(2 * tiles):
-                fitted[i] += dot(inc, zt_all[i, rows, :])
+                fitted[i] += dot(inc, zt_all[i, k * fp:(k + 1) * fp, :])
         for q in range(chunks):
             @pl.when(s > 0)
             def _():
@@ -199,8 +189,8 @@
             w_copy(x, panel).start()
 
         for j in others:
-            rs_copy(x, j).wait_send()
-            ag_copy(x, j).wait_send()
+            for k in range(PIECES):
+                sum_copy(x, s, j, k).wait_send()
 
     total = dot(t_flat[...].astype(BF16), a_all[:rl, :])
     for h in range(CORES):
@@ -216,14 +206,11 @@
 
     p_copy.wait_recv()
     for x in range(PARTS):
-        send_parts(x, p_first[c, x] + p_land[x])
+        send_parts(x, 0, p_first[c, x] + p_land[x])
 
     @pl.loop(tiles // 2, tiles)
     def _(i):
         zt_all[i] = stage[i].T.astype(BF16)
-
-    add_up(0, 0)
-    add_up(1, 0)
 
     @pl.loop(0, tiles)
     def _(i):
@@ -238,10 +225,8 @@
     def _(s):
         project(0, s)
         update(1, s - 1)
-        add_up(0, s)
         project(1, s)
         update(0, s)
-        add_up(1, s)
 
     update(1, steps - 1)
 
@@ -278,11 +263,11 @@
     rl, fb = features.shape
     width = targets.shape[0]
     half = width // (CORES * PARTS)
-    fs = fb // nz
+    fs, fp = fb // nz, fb // PIECES
     tiles, own_chunks = rl // TILE, rl // CHUNK
     chunks, steps = 2 * own_chunks, TURNS * nb
     dma = pltpu.SemaphoreType.DMA
-    hbm = pl.BlockSpec(memory_space=pl.ANY)
+    hbm = pl.BlockSpec(memory_space=pltpu.HBM)
     vmem = pl.BlockSpec(memory_space=pltpu.VMEM)
     weights, residual = pl.pallas_call(
         functools.partial(kernel, nz, nb),
@@ -300,27 +285,25 @@
             pltpu.VMEM((tiles, TILE, fb), F32),
             pltpu.VMEM((tiles, TILE, fb), F32),
             pltpu.VMEM((fb, fb), BF16),
-            pltpu.VMEM((fb, fs), BF16),
-            pltpu.VMEM((fb, fs), BF16),
+            pltpu.VMEM((fs, fb), BF16),
+            pltpu.VMEM((fs, fb), BF16),
             pltpu.VMEM((2 * rl, fb), BF16),
             pltpu.VMEM((2 * tiles, fb, TILE), BF16),
             pltpu.VMEM((steps + 1, PARTS, chunks, half, CHUNK), F32),
             pltpu.VMEM((PARTS, own_chunks, half, CHUNK), F32),
-            pltpu.VMEM((PARTS, nz, half, fs), F32),
-            pltpu.VMEM((PARTS, nz, half, fs), F32),
-            pltpu.VMEM((PARTS, nz, half, fs), F32),
+            pltpu.VMEM((PARTS, half, fb), F32),
+            pltpu.VMEM((2, PARTS, nz, PIECES, half, fp), F32),
             pltpu.VMEM((nb, PARTS, nz, half, fs), F32),
             pltpu.VMEM((nb, PARTS, nz, half, fs), F32),
             dma((tiles,)), dma((tiles,)),
             dma((PARTS, own_chunks)), dma((PARTS, own_chunks)),
             dma((PARTS, chunks)), dma((steps + 1, PARTS, chunks)),
-            dma((PARTS, nz)), dma((PARTS, nz)),
-            dma((PARTS, nz)), dma((PARTS, nz)),
+            dma((PARTS, nz, PIECES)), dma((2, PARTS, nz, PIECES)),
             dma((nb, PARTS)), dma((nb, PARTS)),
             dma((tiles + 1,)), dma, dma,
         ],
         compiler_params=pltpu.CompilerParams(
-            collective_id=0, has_side_effects=True, vmem_limit_bytes=50 * 2**20
+            collective_id=0, has_side_effects=True, vmem_limit_bytes=60 * 2**20
         ),
     )(features, inverse_gram, targets.reshape(CORES, PARTS, half, rl), targets)
     return weights.reshape(nb * width, fb), residual.reshape(width, rl)

time: 117 us -> 98.8 us (0.84)
  Pallas kernels: 113 us -> 94.5 us
    pallas_call x1, Pallas kernels: 113 us -> 94.5 us  [local(): pl.pallas_call(functools.partial(kernel, nz, nb), out_shape=(jax.ShapeDty...]
    unnamed x6 -> x2, local copies, waits for them, and re-layouts: 3.94 us -> 3.45 us
where the time goes in v4:
time: 98.8 us; the launch traced here: 98.6 us
  Pallas kernels  94.5 us (96%)
  local copies, waits for them, and re-layouts  3.45 us (3%)
    pallas_call x1, Pallas kernels, local(): pl.pallas_call(functools.partial(kernel, nz, nb), out_shape=(jax.ShapeDty...  94.5 us
    unnamed x2, local copies, waits for them, and re-layouts  3.45 us

profile of v4, /device:TPU:0, one launch (start us, length us, event | category | flops | bytes accessed | tf_op | source)
XLA Modules:
  0.0 98.6 jit_solution(17194917846067436784)
XLA Ops:
  0.6 94.5 %shard_map.50 = (f32[4,2,2,8,1024]{4,3,2,1,0:T(8,128)}, f32[2,2,8,1024]{3,2,1,0:T(8,128)}) custom-call(bf16[1024,1024]{1,0:T(8,128)(2,1)} %z_hbm.1, f32[1024,1024]{1,0:T(8,128)} %g_hbm.1, f32[2,2,8,1024]{3,2,1,0:T(8,128)} %bitcast.3, f32[32,1024]{1,0:T(8,128)} %t_flat.1), custom_call_target="tpu_custom_call" | custom-call | tf_op jit(solution)/shard_map/pallas_call | solution.py:272
  95.1 1.9 %copy.7 = f32[128,1024]{1,0:T(8,128)} copy(f32[128,1024]{1,0:T(8,128)} %bitcast.4) | data formatting | bytes 1048576
  97.0 1.6 %copy.8 = f32[32,1024]{1,0:T(8,128)} copy(f32[32,1024]{1,0:T(8,128)} %bitcast.5) | data formatting | bytes 262144

commit v5 on v4

--- a/solution.py
+++ b/solution.py
@@ -45,7 +45,6 @@
     tiles = rl // TILE
     own_chunks = rl // CHUNK
     chunks = 2 * own_chunks
-    per_chunk = CHUNK // TILE
 
     def chip(j):
         return {"rows": j * CORES + c, "feat": f}
@@ -103,10 +102,13 @@
     w_own[...] = jnp.zeros_like(w_own)
     pull[...] = jnp.zeros_like(pull)
 
+    def turned(tile, values):
+        zt_all[:, pl.ds(pl.multiple_of(tile * TILE, TILE), TILE)] = values.T
+
     def prepare(tile, values):
         rows = pl.ds(pl.multiple_of(tile * TILE, TILE), TILE)
-        a_all[rows, :] = dot(values.astype(BF16), gb[...]).astype(BF16)
-        zt_all[tile] = values.T.astype(BF16)
+        a_all[rows, :] = dot(values, gb[...]).astype(BF16)
+        turned(tile, values)
 
     @pl.loop(0, tiles)
     def _(i):
@@ -163,7 +165,7 @@
 
     def update(x, s):
         panel = panel_at(s)
-        fitted = [jnp.zeros((half, TILE), F32) for _ in range(2 * tiles)]
+        fitted = jnp.zeros((half, 2 * rl), F32)
         for k in range(PIECES):
             for j in others:
                 sum_wait(x, s, j, k)
@@ -172,16 +174,13 @@
                 inc += sums[lax.rem(s, 2), x, j, k]
             for j in range(fp // fs):
                 w_own[panel, x, k * (fp // fs) + j] += inc[:, j * fs:(j + 1) * fs]
-            inc = inc.astype(BF16)
-            for i in range(2 * tiles):
-                fitted[i] += dot(inc, zt_all[i, k * fp:(k + 1) * fp, :])
+            fitted += dot(inc.astype(BF16), zt_all[k * fp:(k + 1) * fp, :])
         for q in range(chunks):
             @pl.when(s > 0)
             def _():
                 r_copy(x, s - 1, q).wait_send()
 
-            for i in range(per_chunk):
-                res[s, x, q, :, i * TILE:(i + 1) * TILE] -= fitted[q * per_chunk + i]
+            res[s, x, q] -= fitted[:, q * CHUNK:(q + 1) * CHUNK]
             r_copy(x, s, q).start()
 
         @pl.when(s >= steps - nb)
@@ -202,7 +201,7 @@
 
     @pl.loop(0, tiles // 2)
     def _(i):
-        zt_all[i] = stage[i].T.astype(BF16)
+        turned(i, z_own[i])
 
     p_copy.wait_recv()
     for x in range(PARTS):
@@ -210,25 +209,24 @@
 
     @pl.loop(tiles // 2, tiles)
     def _(i):
-        zt_all[i] = stage[i].T.astype(BF16)
+        turned(i, z_own[i])
 
     @pl.loop(0, tiles)
     def _(i):
         z_copy(i).wait_recv()
-        prepare(tiles + i, landed[i])
+        prepare(tiles + i, landed[i].astype(BF16))
 
     for x, q in both:
         t_copy(x, q).wait_recv()
-    update(0, 0)
+    for x in range(PARTS):
+        update(x, 0)
 
     @pl.loop(1, steps)
     def _(s):
-        project(0, s)
-        update(1, s - 1)
-        project(1, s)
-        update(0, s)
-
-    update(1, steps - 1)
+        for x in range(PARTS):
+            project(x, s)
+        for x in range(PARTS):
+            update(x, s)
 
     for x, q in both:
         for h, k in ((c, q), (1 - c, own_chunks + q)):
@@ -288,7 +286,7 @@
             pltpu.VMEM((fs, fb), BF16),
             pltpu.VMEM((fs, fb), BF16),
             pltpu.VMEM((2 * rl, fb), BF16),
-            pltpu.VMEM((2 * tiles, fb, TILE), BF16),
+            pltpu.VMEM((fb, 2 * rl), BF16),
             pltpu.VMEM((steps + 1, PARTS, chunks, half, CHUNK), F32),
             pltpu.VMEM((PARTS, own_chunks, half, CHUNK), F32),
             pltpu.VMEM((PARTS, half, fb), F32),
@@ -303,7 +301,7 @@
             dma((tiles + 1,)), dma, dma,
         ],
         compiler_params=pltpu.CompilerParams(
-            collective_id=0, has_side_effects=True, vmem_limit_bytes=60 * 2**20
+            collective_id=0, has_side_effects=True, vmem_limit_bytes=50 * 2**20
         ),
     )(features, inverse_gram, targets.reshape(CORES, PARTS, half, rl), targets)
     return weights.reshape(nb * width, fb), residual.reshape(width, rl)

time: 98.8 us -> 97.2 us (0.984)
  Pallas kernels: 94.5 us -> 91.6 us
    pallas_call x1, Pallas kernels: 94.5 us -> 91.6 us  [local(): pl.pallas_call(functools.partial(kernel, nz, nb), out_shape=(jax.ShapeDty...]
    unnamed x2 -> x6, local copies, waits for them, and re-layouts: 3.45 us -> 3.94 us
where the time goes in v5:
time: 97.2 us; the launch traced here: 96.2 us
  Pallas kernels  91.6 us (94%)
  local copies, waits for them, and re-layouts  3.94 us (4%)
    pallas_call x1, Pallas kernels, local(): pl.pallas_call(functools.partial(kernel, nz, nb), out_shape=(jax.ShapeDty...  91.6 us
    unnamed x6, local copies, waits for them, and re-layouts  3.94 us

profile of v5, /device:TPU:0, one launch (start us, length us, event | category | flops | bytes accessed | tf_op | source)
XLA Modules:
  0.0 96.2 jit_solution(6303488150184079841)
XLA Ops:
  0.6 0.0 copy-start
  0.6 1.6 %copy-done = bf16[1024,1024]{1,0:T(8,128)(2,1)S(1)} copy-done((bf16[1024,1024]{1,0:T(8,128)(2,1)S(1)}, bf16[1024,1024]{1,0:T(8,128)(2,1)}, u32[]{:S(2)}) %copy-start) | copy-done | bytes 2097176
  2.2 0.0 copy-start.1
  2.2 0.9 copy-done.1
  3.1 91.6 %shard_map.50 = (f32[4,2,2,8,1024]{4,3,2,1,0:T(8,128)S(1)}, f32[2,2,8,1024]{3,2,1,0:T(8,128)S(1)}) custom-call(bf16[1024,1024]{1,0:T(8,128)(2,1)S(1)} %copy-done, f32[1024,1024]{1,0:T(8,128)} %g_hbm.1, f32[2,2,8,1024]{3,2,1,0:T(8,128)S(1)} %bitcast.3, f32[32,1024]{1,0:T(8,128)S(1)} %copy-done.1), custom_call_target="tpu_custom_call" | custom-call | tf_op jit(solution)/shard_map/pallas_call | solution.py:270
  94.7 0.8 copy.7
  95.5 0.7 copy.8
Async XLA Ops:
  0.6 1.6 %copy-start = (bf16[1024,1024]{1,0:T(8,128)(2,1)S(1)}, bf16[1024,1024]{1,0:T(8,128)(2,1)}, u32[]{:S(2)}) copy-start(bf16[1024,1024]{1,0:T(8,128)(2,1)} %z_hbm.1) | copy-start | bytes 6291460
  2.2 0.9 copy-start.1

commit v6 on v5

--- a/solution.py
+++ b/solution.py
@@ -82,38 +82,18 @@
             t_stage.at[x, q], res.at[0, x, own_chunks + q], t_s.at[x, q], t_r.at[x, q], mate
         )
 
-    for x, q in both:
-        t_stage[x, q] = t_ref[1 - c, x, :, q * CHUNK:(q + 1) * CHUNK]
-        t_copy(x, q).start()
-
     @pl.loop(0, tiles)
     def _(i):
         load_z(i).wait()
         stage[i] = z_own[i].astype(F32)
         z_copy(i).start()
 
-    load_g.wait()
-    gb[...] = g_ref[...].astype(BF16)
-    g_mine = g_ref[pl.ds(pl.multiple_of(z * fs, fs), fs), :]
-    gs_hi[...] = g_mine.astype(BF16)
-    gs_lo[...] = (g_mine - g_mine.astype(BF16).astype(F32)).astype(BF16)
-    for x, q in both:
-        res[0, x, q] = t_ref[c, x, :, q * CHUNK:(q + 1) * CHUNK]
-    w_own[...] = jnp.zeros_like(w_own)
-    pull[...] = jnp.zeros_like(pull)
-
     def turned(tile, values):
         zt_all[:, pl.ds(pl.multiple_of(tile * TILE, TILE), TILE)] = values.T
 
     def prepare(tile, values):
         rows = pl.ds(pl.multiple_of(tile * TILE, TILE), TILE)
         a_all[rows, :] = dot(values, gb[...]).astype(BF16)
-        turned(tile, values)
-
-    @pl.loop(0, tiles)
-    def _(i):
-        rows = pl.ds(pl.multiple_of(i * TILE, TILE), TILE)
-        a_all[rows, :] = dot(z_own[i], gb[...]).astype(BF16)
 
     def r_copy(x, s, q):
         home = lax.div(s, steps - 1) * (q // own_chunks)
@@ -163,23 +143,31 @@
             total += dot(res[s, x, q].astype(BF16), a_all[q * CHUNK:(q + 1) * CHUNK, :])
         send_parts(x, s, total)
 
-    def update(x, s):
+    def update(x, s, first=False):
         panel = panel_at(s)
+        if not first:
+            for q in range(chunks):
+                r_copy(x, s - 1, q).wait_send()
+
+        def summed(k):
+            for j in others:
+                sum_wait(x, s, j, k)
+            value = sums[lax.rem(s, 2), x, 0, k]
+            for j in range(1, nz):
+                value += sums[lax.rem(s, 2), x, j, k]
+            return value
+
+        if first:
+            whole = jnp.zeros((half, fb), F32)
+            for k in range(PIECES):
+                whole += dot(summed(k).astype(BF16), gb[k * fp:(k + 1) * fp, :])
         fitted = jnp.zeros((half, 2 * rl), F32)
         for k in range(PIECES):
-            for j in others:
-                sum_wait(x, s, j, k)
-            inc = sums[lax.rem(s, 2), x, 0, k]
-            for j in range(1, nz):
-                inc += sums[lax.rem(s, 2), x, j, k]
+            inc = whole[:, k * fp:(k + 1) * fp] if first else summed(k)
             for j in range(fp // fs):
                 w_own[panel, x, k * (fp // fs) + j] += inc[:, j * fs:(j + 1) * fs]
             fitted += dot(inc.astype(BF16), zt_all[k * fp:(k + 1) * fp, :])
         for q in range(chunks):
-            @pl.when(s > 0)
-            def _():
-                r_copy(x, s - 1, q).wait_send()
-
             res[s, x, q] -= fitted[:, q * CHUNK:(q + 1) * CHUNK]
             r_copy(x, s, q).start()
 
@@ -191,7 +179,9 @@
             for k in range(PIECES):
                 sum_copy(x, s, j, k).wait_send()
 
-    total = dot(t_flat[...].astype(BF16), a_all[:rl, :])
+    total = jnp.zeros((t_flat.shape[0], fb), F32)
+    for i in range(tiles):
+        total += dot(t_flat[:, i * TILE:(i + 1) * TILE].astype(BF16), z_own[i])
     for h in range(CORES):
         for x in range(PARTS):
             first = (h * PARTS + x) * half
@@ -199,27 +189,42 @@
     p_copy = remote(p_first.at[1 - c], p_land, p_s, p_r, mate)
     p_copy.start()
 
-    @pl.loop(0, tiles // 2)
-    def _(i):
-        turned(i, z_own[i])
+    for x, q in both:
+        t_stage[x, q] = t_ref[1 - c, x, :, q * CHUNK:(q + 1) * CHUNK]
+        t_copy(x, q).start()
 
     p_copy.wait_recv()
     for x in range(PARTS):
         send_parts(x, 0, p_first[c, x] + p_land[x])
 
-    @pl.loop(tiles // 2, tiles)
-    def _(i):
+    load_g.wait()
+    gb[...] = g_ref[...].astype(BF16)
+    g_mine = g_ref[pl.ds(pl.multiple_of(z * fs, fs), fs), :]
+    gs_hi[...] = g_mine.astype(BF16)
+    gs_lo[...] = (g_mine - g_mine.astype(BF16).astype(F32)).astype(BF16)
+    for x, q in both:
+        res[0, x, q] = t_ref[c, x, :, q * CHUNK:(q + 1) * CHUNK]
+    w_own[...] = jnp.zeros_like(w_own)
+    pull[...] = jnp.zeros_like(pull)
+
+    @pl.loop(0, tiles)
+    def _(i):
+        prepare(i, z_own[i])
         turned(i, z_own[i])
 
     @pl.loop(0, tiles)
     def _(i):
         z_copy(i).wait_recv()
-        prepare(tiles + i, landed[i].astype(BF16))
+        turned(tiles + i, landed[i].astype(BF16))
 
     for x, q in both:
         t_copy(x, q).wait_recv()
     for x in range(PARTS):
-        update(x, 0)
+        update(x, 0, True)
+
+    @pl.loop(0, tiles)
+    def _(i):
+        prepare(tiles + i, landed[i].astype(BF16))
 
     @pl.loop(1, steps)
     def _(s):

time: 97.2 us -> 97.3 us (level)
  no operation moved by 1% of the time
where the time goes in v6:
time: 97.3 us; the launch traced here: 97.1 us
  Pallas kernels  92.5 us (95%)
  local copies, waits for them, and re-layouts  3.94 us (4%)
    pallas_call x1, Pallas kernels, local(): pl.pallas_call(functools.partial(kernel, nz, nb), out_shape=(jax.ShapeDty...  92.5 us
    unnamed x6, local copies, waits for them, and re-layouts  3.94 us

profile of v6, /device:TPU:0, one launch (start us, length us, event | category | flops | bytes accessed | tf_op | source)
XLA Modules:
  0.0 97.1 jit_solution(3987016238643588672)
XLA Ops:
  0.6 0.0 copy-start
  0.6 1.6 %copy-done = bf16[1024,1024]{1,0:T(8,128)(2,1)S(1)} copy-done((bf16[1024,1024]{1,0:T(8,128)(2,1)S(1)}, bf16[1024,1024]{1,0:T(8,128)(2,1)}, u32[]{:S(2)}) %copy-start) | copy-done | bytes 2097176
  2.2 0.0 copy-start.1
  2.2 0.9 copy-done.1
  3.1 92.5 %shard_map.50 = (f32[4,2,2,8,1024]{4,3,2,1,0:T(8,128)S(1)}, f32[2,2,8,1024]{3,2,1,0:T(8,128)S(1)}) custom-call(bf16[1024,1024]{1,0:T(8,128)(2,1)S(1)} %copy-done, f32[1024,1024]{1,0:T(8,128)} %g_hbm.1, f32[2,2,8,1024]{3,2,1,0:T(8,128)S(1)} %bitcast.3, f32[32,1024]{1,0:T(8,128)S(1)} %copy-done.1), custom_call_target="tpu_custom_call" | custom-call | tf_op jit(solution)/shard_map/pallas_call | solution.py:275
  95.6 0.8 copy.7
  96.4 0.7 copy.8
Async XLA Ops:
  0.6 1.6 %copy-start = (bf16[1024,1024]{1,0:T(8,128)(2,1)S(1)}, bf16[1024,1024]{1,0:T(8,128)(2,1)}, u32[]{:S(2)}) copy-start(bf16[1024,1024]{1,0:T(8,128)(2,1)} %z_hbm.1) | copy-start | bytes 6291460
  2.2 0.9 copy-start.1

commit v7 on v6

--- a/solution.py
+++ b/solution.py
@@ -25,10 +25,10 @@
 
 def kernel(
     nz, nb,
-    z_hbm, g_hbm, t_ref, t_flat, w_out, r_out,
-    z_own, g_ref, p_first, p_land, stage, landed, gb, gs_hi, gs_lo, a_all, zt_all, res, t_stage,
+    z_hbm, g_hbm, t_ref, w_out, r_out,
+    z_own, g_ref, p_first, p_land, stage, landed, gb, gs_hi, gs_lo, a_all, zt_all, res, i_first, r_first,
     pull, sums, w_own, w_other,
-    z_s, z_r, t_s, t_r, r_s, r_r, sum_s, sum_r, w_s, w_r, in_s, p_s, p_r,
+    z_s, z_r, i_s, i_r, r_s, r_r, sum_s, sum_r, w_s, w_r, in_s, p_s, p_r,
 ):
     row, f = lax.axis_index("rows"), lax.axis_index("feat")
     z, c = lax.div(row, CORES), lax.rem(row, CORES)
@@ -39,7 +39,7 @@
     mate_ahead = {"rows": mate["rows"], "feat": ahead["feat"]}
     mate_behind = {"rows": mate["rows"], "feat": behind["feat"]}
     rl, fb = z_hbm.shape
-    half = t_ref.shape[2]
+    half = t_ref.shape[0] // (CORES * PARTS)
     fs, fp = fb // nz, fb // PIECES
     steps = TURNS * nb
     tiles = rl // TILE
@@ -75,18 +75,11 @@
     def z_copy(i):
         return remote(stage.at[i], landed.at[i], z_s.at[i], z_r.at[i], mate)
 
-    both = [(x, q) for x in range(PARTS) for q in range(own_chunks)]
-
-    def t_copy(x, q):
-        return remote(
-            t_stage.at[x, q], res.at[0, x, own_chunks + q], t_s.at[x, q], t_r.at[x, q], mate
-        )
+    groups = [(h, x, (h * PARTS + x) * half) for h in range(CORES) for x in range(PARTS)]
 
     @pl.loop(0, tiles)
     def _(i):
         load_z(i).wait()
-        stage[i] = z_own[i].astype(F32)
-        z_copy(i).start()
 
     def turned(tile, values):
         zt_all[:, pl.ds(pl.multiple_of(tile * TILE, TILE), TILE)] = values.T
@@ -143,27 +136,21 @@
             total += dot(res[s, x, q].astype(BF16), a_all[q * CHUNK:(q + 1) * CHUNK, :])
         send_parts(x, s, total)
 
-    def update(x, s, first=False):
+    def summed(x, s, k):
+        for j in others:
+            sum_wait(x, s, j, k)
+        value = sums[lax.rem(s, 2), x, 0, k]
+        for j in range(1, nz):
+            value += sums[lax.rem(s, 2), x, j, k]
+        return value
+
+    def update(x, s):
         panel = panel_at(s)
-        if not first:
-            for q in range(chunks):
-                r_copy(x, s - 1, q).wait_send()
-
-        def summed(k):
-            for j in others:
-                sum_wait(x, s, j, k)
-            value = sums[lax.rem(s, 2), x, 0, k]
-            for j in range(1, nz):
-                value += sums[lax.rem(s, 2), x, j, k]
-            return value
-
-        if first:
-            whole = jnp.zeros((half, fb), F32)
-            for k in range(PIECES):
-                whole += dot(summed(k).astype(BF16), gb[k * fp:(k + 1) * fp, :])
+        for q in range(chunks):
+            r_copy(x, s - 1, q).wait_send()
         fitted = jnp.zeros((half, 2 * rl), F32)
         for k in range(PIECES):
-            inc = whole[:, k * fp:(k + 1) * fp] if first else summed(k)
+            inc = summed(x, s, k)
             for j in range(fp // fs):
                 w_own[panel, x, k * (fp // fs) + j] += inc[:, j * fs:(j + 1) * fs]
             fitted += dot(inc.astype(BF16), zt_all[k * fp:(k + 1) * fp, :])
@@ -179,52 +166,74 @@
             for k in range(PIECES):
                 sum_copy(x, s, j, k).wait_send()
 
-    total = jnp.zeros((t_flat.shape[0], fb), F32)
+    total = jnp.zeros((t_ref.shape[0], fb), F32)
     for i in range(tiles):
-        total += dot(t_flat[:, i * TILE:(i + 1) * TILE].astype(BF16), z_own[i])
-    for h in range(CORES):
-        for x in range(PARTS):
-            first = (h * PARTS + x) * half
-            p_first[h, x] = total[first:first + half, :]
+        total += dot(t_ref[:, i * TILE:(i + 1) * TILE].astype(BF16), z_own[i])
+    for h, x, first in groups:
+        p_first[h, x] = total[first:first + half, :]
     p_copy = remote(p_first.at[1 - c], p_land, p_s, p_r, mate)
     p_copy.start()
 
-    for x, q in both:
-        t_stage[x, q] = t_ref[1 - c, x, :, q * CHUNK:(q + 1) * CHUNK]
-        t_copy(x, q).start()
+    @pl.loop(0, tiles)
+    def _(i):
+        stage[i] = z_own[i].astype(F32)
 
     p_copy.wait_recv()
     for x in range(PARTS):
         send_parts(x, 0, p_first[c, x] + p_land[x])
+
+    @pl.loop(0, tiles)
+    def _(i):
+        z_copy(i).start()
 
     load_g.wait()
     gb[...] = g_ref[...].astype(BF16)
     g_mine = g_ref[pl.ds(pl.multiple_of(z * fs, fs), fs), :]
     gs_hi[...] = g_mine.astype(BF16)
     gs_lo[...] = (g_mine - g_mine.astype(BF16).astype(F32)).astype(BF16)
-    for x, q in both:
-        res[0, x, q] = t_ref[c, x, :, q * CHUNK:(q + 1) * CHUNK]
     w_own[...] = jnp.zeros_like(w_own)
     pull[...] = jnp.zeros_like(pull)
 
     @pl.loop(0, tiles)
     def _(i):
+        turned(i, z_own[i])
         prepare(i, z_own[i])
-        turned(i, z_own[i])
+
+    def i_copy(x, h):
+        return remote(i_first.at[h, x], i_first.at[h, x], i_s.at[x], i_r.at[x], mate)
+
+    for x in range(PARTS):
+        inc = jnp.zeros((half, fb), F32)
+        for k in range(PIECES):
+            inc += dot(summed(x, 0, k).astype(BF16), gb[k * fp:(k + 1) * fp, :])
+        i_first[c, x] = inc
+        i_copy(x, c).start()
+        for j in range(nz):
+            w_own[panel_at(0), x, j] = inc[:, j * fs:(j + 1) * fs]
+    for x in range(PARTS):
+        i_copy(x, 1 - c).wait_recv()
+    inc = jnp.concatenate([i_first[h, x] for h, x, _ in groups], axis=0)
+    left = t_ref[...] - dot(inc.astype(BF16), zt_all[:, :rl])
+    for h, x, first in groups:
+        for q in range(own_chunks):
+            r_first[h, x, q] = left[first:first + half, q * CHUNK:(q + 1) * CHUNK]
+    for x in range(PARTS):
+        for q in range(own_chunks):
+            for h, k, device in ((c, q, ahead), (1 - c, own_chunks + q, mate_ahead)):
+                remote(
+                    r_first.at[h, x, q], res.at[1, x, k], r_s.at[x, k], r_r.at[1, x, k], device
+                ).start()
+    for x in range(PARTS):
+        for j in others:
+            for k in range(PIECES):
+                sum_copy(x, 0, j, k).wait_send()
 
     @pl.loop(0, tiles)
     def _(i):
         z_copy(i).wait_recv()
-        turned(tiles + i, landed[i].astype(BF16))
-
-    for x, q in both:
-        t_copy(x, q).wait_recv()
-    for x in range(PARTS):
-        update(x, 0, True)
-
-    @pl.loop(0, tiles)
-    def _(i):
-        prepare(tiles + i, landed[i].astype(BF16))
+        values = landed[i].astype(BF16)
+        prepare(tiles + i, values)
+        turned(tiles + i, values)
 
     @pl.loop(1, steps)
     def _(s):
@@ -233,7 +242,7 @@
         for x in range(PARTS):
             update(x, s)
 
-    for x, q in both:
+    for x, q in [(x, q) for x in range(PARTS) for q in range(own_chunks)]:
         for h, k in ((c, q), (1 - c, own_chunks + q)):
             r_copy(x, steps - 1, k).wait_recv()
             r_out[h, x, :, q * CHUNK:(q + 1) * CHUNK] = res[steps, x, k]
@@ -249,8 +258,8 @@
             w_copy(x, panel).wait_send()
 
     p_copy.wait_send()
-    for x, q in both:
-        t_copy(x, q).wait_send()
+    for x in range(PARTS):
+        i_copy(x, c).wait_send()
     for x in range(PARTS):
         for q in range(chunks):
             r_copy(x, steps - 1, q).wait_send()
@@ -278,7 +287,7 @@
             jax.ShapeDtypeStruct((nb, CORES, PARTS, half, fb), F32),
             jax.ShapeDtypeStruct((CORES, PARTS, half, rl), F32),
         ),
-        in_specs=[hbm, hbm, vmem, vmem],
+        in_specs=[hbm, hbm, vmem],
         out_specs=(vmem, vmem),
         scratch_shapes=[
             pltpu.VMEM((tiles, TILE, fb), BF16),
@@ -293,13 +302,14 @@
             pltpu.VMEM((2 * rl, fb), BF16),
             pltpu.VMEM((fb, 2 * rl), BF16),
             pltpu.VMEM((steps + 1, PARTS, chunks, half, CHUNK), F32),
-            pltpu.VMEM((PARTS, own_chunks, half, CHUNK), F32),
+            pltpu.VMEM((CORES, PARTS, half, fb), F32),
+            pltpu.VMEM((CORES, PARTS, own_chunks, half, CHUNK), F32),
             pltpu.VMEM((PARTS, half, fb), F32),
             pltpu.VMEM((2, PARTS, nz, PIECES, half, fp), F32),
             pltpu.VMEM((nb, PARTS, nz, half, fs), F32),
             pltpu.VMEM((nb, PARTS, nz, half, fs), F32),
             dma((tiles,)), dma((tiles,)),
-            dma((PARTS, own_chunks)), dma((PARTS, own_chunks)),
+            dma((PARTS,)), dma((PARTS,)),
             dma((PARTS, chunks)), dma((steps + 1, PARTS, chunks)),
             dma((PARTS, nz, PIECES)), dma((2, PARTS, nz, PIECES)),
             dma((nb, PARTS)), dma((nb, PARTS)),
@@ -308,7 +318,7 @@
         compiler_params=pltpu.CompilerParams(
             collective_id=0, has_side_effects=True, vmem_limit_bytes=50 * 2**20
         ),
-    )(features, inverse_gram, targets.reshape(CORES, PARTS, half, rl), targets)
+    )(features, inverse_gram, targets)
     return weights.reshape(nb * width, fb), residual.reshape(width, rl)
 
 

time: 97.3 us -> 92.6 us (0.952)
  Pallas kernels: 92.5 us -> 87.8 us
    pallas_call x1, Pallas kernels: 92.5 us -> 87.8 us  [local(): pl.pallas_call(functools.partial(kernel, nz, nb), out_shape=(jax.ShapeDty...]
where the time goes in v7:
time: 92.6 us; the launch traced here: 92.4 us
  Pallas kernels  87.8 us (95%)
  local copies, waits for them, and re-layouts  3.94 us (4%)
    pallas_call x1, Pallas kernels, local(): pl.pallas_call(functools.partial(kernel, nz, nb), out_shape=(jax.ShapeDty...  87.8 us
    unnamed x6, local copies, waits for them, and re-layouts  3.94 us

profile of v7, /device:TPU:0, one launch (start us, length us, event | category | flops | bytes accessed | tf_op | source)
XLA Modules:
  0.0 92.4 jit_solution(16809083156956093802)
XLA Ops:
  0.6 0.0 copy-start
  0.6 1.6 %copy-done = bf16[1024,1024]{1,0:T(8,128)(2,1)S(1)} copy-done((bf16[1024,1024]{1,0:T(8,128)(2,1)S(1)}, bf16[1024,1024]{1,0:T(8,128)(2,1)}, u32[]{:S(2)}) %copy-start) | copy-done | bytes 2097176
  2.2 0.0 copy-start.1
  2.2 0.9 copy-done.1
  3.1 87.8 %shard_map.50 = (f32[4,2,2,8,1024]{4,3,2,1,0:T(8,128)S(1)}, f32[2,2,8,1024]{3,2,1,0:T(8,128)S(1)}) custom-call(bf16[1024,1024]{1,0:T(8,128)(2,1)S(1)} %copy-done, f32[1024,1024]{1,0:T(8,128)} %g_hbm.1, f32[32,1024]{1,0:T(8,128)S(1)} %copy-done.1), custom_call_target="tpu_custom_call" | custom-call | tf_op jit(solution)/shard_map/pallas_call | solution.py:284
  91.0 0.8 copy.7
  91.8 0.7 copy.8
Async XLA Ops:
  0.6 1.6 %copy-start = (bf16[1024,1024]{1,0:T(8,128)(2,1)S(1)}, bf16[1024,1024]{1,0:T(8,128)(2,1)}, u32[]{:S(2)}) copy-start(bf16[1024,1024]{1,0:T(8,128)(2,1)} %z_hbm.1) | copy-start | bytes 6291460
  2.2 0.9 copy-start.1

commit v8 on v7

--- a/solution.py
+++ b/solution.py
@@ -35,7 +35,9 @@
     mate = {"rows": z * CORES + (CORES - 1 - c), "feat": f}
     ahead = {"rows": row, "feat": lax.rem(f + 1, nb)}
     behind = {"rows": row, "feat": lax.rem(f + nb - 1, nb)}
-    others = [lax.rem(z + d, nz) for d in range(1, nz)]
+    side = 1 - 2 * lax.rem(z, 2)
+    turns = [0] + [e for d in range(1, nz // 2) for e in (d, -d)]
+    others = [lax.rem(z + nz // 2 + nz + side * e, nz) for e in turns]
     mate_ahead = {"rows": mate["rows"], "feat": ahead["feat"]}
     mate_behind = {"rows": mate["rows"], "feat": behind["feat"]}
     rl, fb = z_hbm.shape
@@ -113,11 +115,10 @@
     def panel_at(s):
         return lax.rem(f + steps - s, nb)
 
-    def send_parts(x, s, total):
-        for k in range(PIECES):
-            sums[lax.rem(s, 2), x, z, k] = total[:, k * fp:(k + 1) * fp]
-            for j in others:
-                sum_copy(x, s, j, k).start()
+    def send_piece(x, s, k, value):
+        sums[lax.rem(s, 2), x, z, k] = value
+        for j in others:
+            sum_copy(x, s, j, k).start()
 
     def project(x, s):
         panel = panel_at(s)
@@ -130,11 +131,16 @@
             hi, lo = gs_hi[...], gs_lo[...]
             pull[x] = ridge_weight * (dot(w_hi, hi) + dot(w_lo, hi) + dot(w_hi, lo))
 
-        total = -pull[x]
+        totals = [-pull[x, :, k * fp:(k + 1) * fp] for k in range(PIECES)]
         for q in range(chunks):
             r_copy(x, s - 1, q).wait_recv()
-            total += dot(res[s, x, q].astype(BF16), a_all[q * CHUNK:(q + 1) * CHUNK, :])
-        send_parts(x, s, total)
+            rows = res[s, x, q].astype(BF16)
+            for k in range(PIECES):
+                totals[k] += dot(
+                    rows, a_all[q * CHUNK:(q + 1) * CHUNK, k * fp:(k + 1) * fp]
+                )
+                if q == chunks - 1:
+                    send_piece(x, s, k, totals[k])
 
     def summed(x, s, k):
         for j in others:
@@ -148,15 +154,19 @@
         panel = panel_at(s)
         for q in range(chunks):
             r_copy(x, s - 1, q).wait_send()
-        fitted = jnp.zeros((half, 2 * rl), F32)
+        fitted = [jnp.zeros((half, CHUNK), F32) for _ in range(chunks)]
         for k in range(PIECES):
             inc = summed(x, s, k)
             for j in range(fp // fs):
                 w_own[panel, x, k * (fp // fs) + j] += inc[:, j * fs:(j + 1) * fs]
-            fitted += dot(inc.astype(BF16), zt_all[k * fp:(k + 1) * fp, :])
-        for q in range(chunks):
-            res[s, x, q] -= fitted[:, q * CHUNK:(q + 1) * CHUNK]
-            r_copy(x, s, q).start()
+            inc = inc.astype(BF16)
+            for q in range(chunks):
+                fitted[q] += dot(
+                    inc, zt_all[k * fp:(k + 1) * fp, q * CHUNK:(q + 1) * CHUNK]
+                )
+                if k == PIECES - 1:
+                    res[s, x, q] -= fitted[q]
+                    r_copy(x, s, q).start()
 
         @pl.when(s >= steps - nb)
         def _():
@@ -180,7 +190,9 @@
 
     p_copy.wait_recv()
     for x in range(PARTS):
-        send_parts(x, 0, p_first[c, x] + p_land[x])
+        for k in range(PIECES):
+            cols = slice(k * fp, (k + 1) * fp)
+            send_piece(x, 0, k, p_first[c, x, :, cols] + p_land[x, :, cols])
 
     @pl.loop(0, tiles)
     def _(i):

time: 92.6 us -> 95.4 us (1.030)
  Pallas kernels: 87.8 us -> 90.6 us
    pallas_call x1, Pallas kernels: 87.8 us -> 90.6 us  [local(): pl.pallas_call(functools.partial(kernel, nz, nb), out_shape=(jax.ShapeDty...]
where the time goes in v8:
time: 95.4 us; the launch traced here: 95.2 us
  Pallas kernels  90.6 us (95%)
  local copies, waits for them, and re-layouts  3.94 us (4%)
    pallas_call x1, Pallas kernels, local(): pl.pallas_call(functools.partial(kernel, nz, nb), out_shape=(jax.ShapeDty...  90.6 us
    unnamed x6, local copies, waits for them, and re-layouts  3.94 us

profile of v8, /device:TPU:0, one launch (start us, length us, event | category | flops | bytes accessed | tf_op | source)
XLA Modules:
  0.0 95.2 jit_solution(12438412380462591529)
XLA Ops:
  0.6 0.0 copy-start
  0.6 1.6 %copy-done = bf16[1024,1024]{1,0:T(8,128)(2,1)S(1)} copy-done((bf16[1024,1024]{1,0:T(8,128)(2,1)S(1)}, bf16[1024,1024]{1,0:T(8,128)(2,1)}, u32[]{:S(2)}) %copy-start) | copy-done | bytes 2097176
  2.2 0.0 copy-start.1
  2.2 0.9 copy-done.1
  3.1 90.6 %shard_map.50 = (f32[4,2,2,8,1024]{4,3,2,1,0:T(8,128)S(1)}, f32[2,2,8,1024]{3,2,1,0:T(8,128)S(1)}) custom-call(bf16[1024,1024]{1,0:T(8,128)(2,1)S(1)} %copy-done, f32[1024,1024]{1,0:T(8,128)} %g_hbm.1, f32[32,1024]{1,0:T(8,128)S(1)} %copy-done.1), custom_call_target="tpu_custom_call" | custom-call | tf_op jit(solution)/shard_map/pallas_call | solution.py:296
  93.7 0.8 copy.7
  94.5 0.7 copy.8
Async XLA Ops:
  0.6 1.6 %copy-start = (bf16[1024,1024]{1,0:T(8,128)(2,1)S(1)}, bf16[1024,1024]{1,0:T(8,128)(2,1)}, u32[]{:S(2)}) copy-start(bf16[1024,1024]{1,0:T(8,128)(2,1)} %z_hbm.1) | copy-start | bytes 6291460
  2.2 0.9 copy-start.1

commit v9 on v7

--- a/solution.py
+++ b/solution.py
@@ -12,7 +12,7 @@
 TILE = 256
 PIECES = 2
 PARTS = 2
-CHUNK = 512
+CHUNK = 1024
 
 ridge_weight = 0.5
 MESH = pl.DeviceIdType.MESH

time: 92.6 us -> 92.9 us (level)
  no operation moved by 1% of the time
where the time goes in v9:
time: 92.9 us; the launch traced here: 92.7 us
  Pallas kernels  88.1 us (95%)
  local copies, waits for them, and re-layouts  3.94 us (4%)
    pallas_call x1, Pallas kernels, local(): pl.pallas_call(functools.partial(kernel, nz, nb), out_shape=(jax.ShapeDty...  88.1 us
    unnamed x6, local copies, waits for them, and re-layouts  3.94 us

profile of v9, /device:TPU:0, one launch (start us, length us, event | category | flops | bytes accessed | tf_op | source)
XLA Modules:
  0.0 92.7 jit_solution(11870282714561505585)
XLA Ops:
  0.6 0.0 copy-start
  0.6 1.6 %copy-done = bf16[1024,1024]{1,0:T(8,128)(2,1)S(1)} copy-done((bf16[1024,1024]{1,0:T(8,128)(2,1)S(1)}, bf16[1024,1024]{1,0:T(8,128)(2,1)}, u32[]{:S(2)}) %copy-start) | copy-done | bytes 2097176
  2.2 0.0 copy-start.1
  2.2 0.9 copy-done.1
  3.1 88.1 %shard_map.50 = (f32[4,2,2,8,1024]{4,3,2,1,0:T(8,128)S(1)}, f32[2,2,8,1024]{3,2,1,0:T(8,128)S(1)}) custom-call(bf16[1024,1024]{1,0:T(8,128)(2,1)S(1)} %copy-done, f32[1024,1024]{1,0:T(8,128)} %g_hbm.1, f32[32,1024]{1,0:T(8,128)S(1)} %copy-done.1), custom_call_target="tpu_custom_call" | custom-call | tf_op jit(solution)/shard_map/pallas_call | solution.py:284
  91.3 0.8 copy.7
  92.1 0.7 copy.8
Async XLA Ops:
  0.6 1.6 %copy-start = (bf16[1024,1024]{1,0:T(8,128)(2,1)S(1)}, bf16[1024,1024]{1,0:T(8,128)(2,1)}, u32[]{:S(2)}) copy-start(bf16[1024,1024]{1,0:T(8,128)(2,1)} %z_hbm.1) | copy-start | bytes 6291460
  2.2 0.9 copy-start.1
